TPU v7x, 256 devices: a whole 4x4x8 slice. The times are simulated.
256 devices in a mesh: half: 2 (over x_lo), dom: 16 (over y, x_hi, core), slab: 8 (over z).
Axes of the slice: x: 4 (x_hi: 2, x_lo: 2; x = x_hi * 2 + x_lo), y: 4, z: 8, core: 2. Of those that a mesh axis runs over, the one named last changes fastest.
Arguments:
- images: bfloat16 [2, 128, 384, 384], P('half', 'dom', 'slab'), may hold values from -6 to 6
- orientation: int32 [2, 128], P('half', 'dom'), may hold values from 0 to 511, as said below
- offsets: int32 [2, 128, 2], P('half', 'dom'), may hold values from -16 to 16
- defocus_class: int32 [2, 128], P('half', 'dom'), may hold values from 0 to 15
- defocus: float32 [16], replicated, may hold values from 150 to 900
- ori_slot: int32 [512], replicated, may hold values from 0 to 511, as said below
- half_maps: bfloat16 [2, 512, 384, 384], P('half', 'dom', 'slab'), may hold values from -8 to 8
Outputs:
- scores: float32 [2, 128], P('half', 'dom')
- new_maps: float32 [2, 512, 384, 384], P('half', 'dom', 'slab')
- shell_corr: float32 [267], replicated
Inputs may be any that keep to these rules, and one draw needn't show every extreme that they name: Let owner = ori_slot[orientation[h, p]] // 32. In each block of the 8 particles of one half-set on one index of dom, at most 2 particles share an owner; in each half-set one owner takes exactly 2 particles from every block, and the other owners' counts in a block differ by at most one. `ori_slot`: a permutation of 0 .. 511.
All inputs are finite; a program needn't handle non-finite values.
Results may differ from a plain program's by a relative error of at most 0.0017.
Values may be sent and summed in bfloat16 or wider, within the bound.
A program may use at most 64 MiB of HBM per device.

v0:
```python
import math

import jax
import jax.numpy as jnp
from jax import lax
from jax.sharding import PartitionSpec as P

SHIFTS = 32
NSHELL = 267


def from_partner(value, axis, distance):
    mask = 2**distance
    pairs = [(source, source ^ mask) for source in range(lax.axis_size(axis))]
    return lax.ppermute(value, axis, pairs)


def shell_index(signed_rows, columns, shell_count):
    squared = signed_rows[:, None] * signed_rows[:, None] + columns[None, :] * columns[None, :]
    radius = jnp.floor(jnp.sqrt(squared.astype(jnp.float32))).astype(jnp.int32)
    radius = (
        radius
        - (radius * radius > squared).astype(jnp.int32)
        + ((radius + 1) * (radius + 1) <= squared).astype(jnp.int32)
    )
    return (jnp.clip(radius - 1, 0, shell_count - 1), squared)


def shell_sum(values, shells):
    return jax.ops.segment_sum(values.reshape(-1), shells.reshape(-1), num_segments=NSHELL)


def ctf_table(defocus, squared, box_size):
    gamma_arg = defocus[:, None, None] * (
        squared.astype(jnp.float32)[None] / float(box_size * box_size)
    )
    return -(0.995 * jnp.sin(gamma_arg) + 0.1 * jnp.cos(gamma_arg))


def window_table(frequency, box_size, window_side):
    offsets_in = jnp.arange(window_side, dtype=jnp.int32) - window_side // 2
    phase_idx = jnp.mod(frequency[:, None] * offsets_in[None, :], box_size)
    angles = phase_idx.astype(jnp.float32) * (2.0 * math.pi / box_size)
    return (jnp.cos(angles), jnp.sin(angles))


def column_matrix(cos_x, sin_x):
    top_half = jnp.concatenate([cos_x, sin_x], axis=1)
    low_half = jnp.concatenate([-sin_x, cos_x], axis=1)
    return jnp.concatenate([top_half, low_half], axis=0).astype(jnp.bfloat16)


def row_matrix(cos_y, sin_y):
    return jnp.stack([cos_y, -sin_y], axis=1).astype(jnp.bfloat16)


def power_sum(left_map, right_map, half_cols):
    product = left_map * right_map
    return jnp.sum(product[..., :half_cols] + product[..., half_cols:], axis=0)


def on_device(images, orientation, offsets, defocus_class, defocus, ori_slot, half_maps):
    part_dev = images.shape[1]
    row_count = images.shape[2]
    half_cols = images.shape[3] // 2
    box_size = 2 * half_cols
    owners = lax.axis_size("dom")
    ori_dev = half_maps.shape[1]
    classes = defocus.shape[0]
    slot_cap = max(2, 3 * part_dev // owners)
    slab_pos = lax.axis_index("slab")
    half_pos = lax.axis_index("half")
    row_ids = slab_pos * row_count + jnp.arange(row_count, dtype=jnp.int32)
    signed_rows = jnp.where(row_ids < half_cols, row_ids, row_ids - box_size)
    columns = jnp.arange(half_cols, dtype=jnp.int32)
    shells, squared = shell_index(signed_rows, columns, NSHELL)
    own_maps = half_maps[0]
    own_float = own_maps.astype(jnp.float32)
    own_sq = power_sum(own_float, own_float, half_cols)
    other_maps = from_partner(own_maps, "half", 0)
    other_float = other_maps.astype(jnp.float32)
    cross_part = power_sum(own_float, other_float, half_cols)
    other_sq = power_sum(other_float, other_float, half_cols)
    first_sq = jnp.where(half_pos == 0, own_sq, other_sq)
    second_sq = jnp.where(half_pos == 0, other_sq, own_sq)
    cross_sum, first_sum, second_sum = lax.psum(
        (shell_sum(cross_part, shells), shell_sum(first_sq, shells), shell_sum(second_sq, shells)),
        ("dom", "slab"),
    )
    shell_corr = cross_sum / jnp.sqrt(first_sum * second_sum + 1e-06)
    weight = jnp.take(jnp.maximum(shell_corr, 0.1), shells)
    weight_pair = jnp.concatenate([weight, weight], axis=-1)
    ctf = ctf_table(defocus, squared, box_size)
    cos_x, sin_x = window_table(columns, box_size, SHIFTS)
    cos_y, sin_y = window_table(signed_rows, box_size, SHIFTS)
    col_table = column_matrix(cos_x, sin_x)
    row_table = row_matrix(cos_y, sin_y)
    slots = jnp.take(ori_slot, orientation[0])
    owner = slots // ori_dev
    local_row = slots % ori_dev
    owner_hot = (owner[:, None] == jnp.arange(owners, dtype=jnp.int32)[None, :]).astype(jnp.int32)
    earlier = jnp.cumsum(owner_hot, axis=0) - owner_hot
    rank_in = jnp.sum(earlier * owner_hot, axis=1)
    target = owner * slot_cap + rank_in
    placing = (target[None, :] == jnp.arange(owners * slot_cap, dtype=jnp.int32)[:, None]).astype(
        jnp.bfloat16
    )
    packed = jnp.dot(placing, images[0].reshape(part_dev, -1), preferred_element_type=jnp.float32)
    packed = packed.astype(jnp.bfloat16).reshape(owners, slot_cap, row_count, 2 * half_cols)
    particle_meta = jnp.stack(
        [defocus_class[0], offsets[0, :, 0], offsets[0, :, 1], local_row, jnp.ones_like(local_row)],
        axis=1,
    )
    packed_meta = (
        jnp.zeros((owners * slot_cap, 5), jnp.int32)
        .at[target]
        .set(particle_meta)
        .reshape(owners, slot_cap, 5)
    )
    item_img = lax.all_to_all(packed, "dom", split_axis=0, concat_axis=0, tiled=True)
    item_meta = lax.all_to_all(packed_meta, "dom", split_axis=0, concat_axis=0, tiled=True)
    senders = item_img.shape[0]
    items = item_img.shape[1]
    count = senders * items
    img_float = item_img.reshape(count, row_count, 2 * half_cols).astype(jnp.float32)
    meta_flat = item_meta.reshape(count, 5)
    x_real = img_float[..., :half_cols]
    x_imag = img_float[..., half_cols:]
    phase_idx = jnp.mod(
        columns[None, None, :] * meta_flat[:, 1][:, None, None]
        + signed_rows[None, :, None] * meta_flat[:, 2][:, None, None],
        box_size,
    )
    angles = phase_idx.astype(jnp.float32) * (2.0 * math.pi / box_size)
    cos_t = jnp.cos(angles)
    sin_t = jnp.sin(angles)
    al_real = x_real * cos_t + x_imag * sin_t
    al_imag = x_imag * cos_t - x_real * sin_t
    picks = (meta_flat[:, 3][:, None] == jnp.arange(ori_dev, dtype=jnp.int32)[None, :]).astype(
        jnp.bfloat16
    )
    chosen = jnp.dot(
        picks, own_maps.reshape(ori_dev, -1), preferred_element_type=jnp.float32
    ).reshape(count, row_count, 2 * half_cols)
    class_hot = (meta_flat[:, 0][:, None] == jnp.arange(classes, dtype=jnp.int32)[None, :]).astype(
        jnp.float32
    )
    ctf_rows = jnp.dot(
        class_hot, ctf.reshape(classes, -1), precision=lax.Precision.HIGHEST
    ).reshape(count, row_count, half_cols)
    p_real = chosen[..., :half_cols]
    p_imag = chosen[..., half_cols:]
    prod_real = weight * ctf_rows * (al_real * p_real + al_imag * p_imag)
    prod_imag = weight * ctf_rows * (al_real * p_imag - al_imag * p_real)
    prod = jnp.concatenate([prod_real, prod_imag], axis=-1).astype(jnp.bfloat16)
    section = jnp.dot(
        prod.reshape(-1, 2 * half_cols), col_table, preferred_element_type=jnp.float32
    )
    section = section.astype(jnp.bfloat16).reshape(count, row_count, 2, SHIFTS)
    corr = jnp.einsum("nycj,yci->nji", section, row_table, preferred_element_type=jnp.float32)
    energy = jnp.sum(
        weight * ctf_rows * ctf_rows * (p_real * p_real + p_imag * p_imag), axis=(1, 2)
    )
    contrib = jnp.concatenate([ctf_rows * al_real, ctf_rows * al_imag], axis=-1).astype(
        jnp.bfloat16
    )
    valid = meta_flat[:, 4].astype(jnp.float32)[:, None, None]
    ctf_sq = ctf_rows * ctf_rows * valid
    corr_part, energy_part, contrib, ctf_sq, local_rows = (
        corr.reshape(senders, items, SHIFTS, SHIFTS),
        energy.reshape(senders, items),
        contrib.reshape(senders, items, row_count, 2 * half_cols),
        ctf_sq.reshape(senders, items, row_count, half_cols),
        meta_flat[:, 3].reshape(senders, items),
    )
    corr_total, energy_total = lax.psum((corr_part, energy_part), "slab")
    best = jnp.max(corr_total, axis=(2, 3))
    slot_score = best / jnp.sqrt(energy_total + 1e-06)
    returned = lax.all_to_all(slot_score, "dom", split_axis=0, concat_axis=0, tiled=True)
    scores = jnp.take(returned.reshape(-1), target)[None, :]
    count_all = owners * slot_cap
    local_hot = (
        local_rows.reshape(count_all)[None, :] == jnp.arange(ori_dev, dtype=jnp.int32)[:, None]
    )
    numer = jnp.dot(
        local_hot.astype(jnp.bfloat16),
        contrib.reshape(count_all, -1),
        preferred_element_type=jnp.float32,
    )
    numer = numer.reshape(ori_dev, row_count, 2 * half_cols)
    ctf_sum = jnp.dot(
        local_hot.astype(jnp.float32),
        ctf_sq.reshape(count_all, -1),
        precision=lax.Precision.HIGHEST,
    )
    ctf_sum = ctf_sum.reshape(ori_dev, row_count, half_cols)
    ctf_pair = jnp.concatenate([ctf_sum, ctf_sum], axis=-1)
    new_maps = ((numer + own_float / weight_pair) / (ctf_pair + 1.0 / weight_pair))[None]
    return (scores, new_maps, shell_corr)


def solution(mesh):
    in_specs = (
        P("half", "dom", "slab", None),
        P("half", "dom"),
        P("half", "dom", None),
        P("half", "dom"),
        P(),
        P(),
        P("half", "dom", "slab", None),
    )
    out_specs = (P("half", "dom"), P("half", "dom", "slab", None), P())
    return jax.shard_map(
        on_device, mesh=mesh, in_specs=in_specs, out_specs=out_specs, check_vma=False
    )
```

profile of v0, /device:TPU:16, one launch (start us, length us, event | category | flops | bytes accessed | tf_op | source)
XLA Modules:
  0.0 779.3 jit_solution(12360304176589392269)
XLA Ops:
  12.7 7.0 all-to-all-start
  23.7 1.9 copy.76
  25.6 14.0 %all-to-all-done = s32[16,2,5]{2,1,0:T(2,128)S(1)} async-done(((s32[16,2,5]{2,1,0:T(2,128)}), s32[16,2,5]{2,1,0:T(2,128)S(1)}, u32[]{:S(2)}, u32[]{:S(2)}) %all-to-all-start) | async-done | bytes 672 | tf_op jit(solution)/shard_map/all_to_all | solution.py:121
  40.2 5.8 all-to-all-start.1
  50.1 1.6 slice_reduce_fusion
  53.7 1.9 fusion.21
  55.7 7.2 all-to-all-done.1
  63.3 2.2 fusion.111
  65.5 2.2 convert_multiply_fusion.2
  72.4 64.7 %scatter_custom_fusion.2 = f32[267]{0:T(512)} fusion(s32[9216]{0:T(1024)} %bitcast.134, f32[9216]{0:T(1024)} %reshape.789, f32[]{:T(128)} %constant.136.clone.1), kind=kCustom, calls=%fused_computation.193 | custom fusion | flops 9216 | bytes 1580 | tf_op jit(solution)/shard_map/scatter-add | solution.py:30
  137.2 64.8 %scatter_custom_fusion.1 = f32[267]{0:T(512)} fusion(s32[9216]{0:T(1024)} %bitcast.135, f32[9216]{0:T(1024)} %reshape.781, f32[]{:T(128)} %constant.136.clone.1), kind=kCustom, calls=%fused_computation.195 | custom fusion | flops 9216 | bytes 1580 | tf_op jit(solution)/shard_map/scatter-add | solution.py:30
  203.9 64.2 %scatter_custom_fusion = f32[267]{0:T(512)S(1)} fusion(s32[9216]{0:T(1024)} %bitcast.136, f32[9216]{0:T(1024)S(1)} %reshape.773, f32[]{:T(128)} %constant.136.clone.1), kind=kCustom, calls=%fused_computation.197 | custom fusion | flops 9216 | bytes 1580 | tf_op jit(solution)/shard_map/scatter-add | solution.py:30
  268.2 295.5 %all-reduce = (f32[267]{0:T(512)S(1)}, f32[267]{0:T(512)S(1)}, f32[267]{0:T(512)S(1)}) all-reduce(f32[267]{0:T(512)S(1)} %scatter_custom_fusion, f32[267]{0:T(512)} %scatter_custom_fusion.1, f32[267]{0:T(512)} %scatter_custom_fusion.2), channel_id=1, replica_groups=mesh['half'=2,'dom'=16,'slab'=8] {'dom','slab'}, use_global_device_ids=true, to_apply=%region_4.5 | all-reduce | flops 801 | bytes 6408 | tf_op jit(solution)/shard_map/psum | solution.py:86
  564.3 57.7 %gather_fusion.1 = f32[9216]{0:T(1024)S(1)} fusion(f32[267]{0:T(512)S(1)} %get-tuple-element.32, s32[9216]{0:T(1024)} %broadcast_clamp_fusion), kind=kCustom, calls=%fused_computation.1 | custom fusion | bytes 110592 | tf_op jit(solution)/shard_map/jit(_take)/gather | solution.py:91
  622.9 13.6 %multiply_convert_fusion.1 = (bf16[32,48,192]{2,0,1:T(8,128)(2,1)}, f32[32,48,192]{2,0,1:T(8,128)}, bf16[32,48,192]{2,0,1:T(8,128)(2,1)}, f32[32,48,192]{2,0,1:T...) fusion(f32[32,48,192]{2,1,0:T(8,128)S(1)} %copy-done.3, s32[32,48]{0,1:T(8,128)S(1)} %copy-done.9, ...), kind=kOutput, calls=%fused_computation.37 | convolution fusion | flops 63554048 | bytes 8325440 | tf_op jit(solution)/shard_map/dot_general | solution.py:148
  637.4 1.6 reshape_reshape.4
  639.1 3.3 dot_general.50
  642.4 4.2 fusion.3
  650.0 3.0 fusion.12
  653.1 14.4 %psum.39 = f32[16,2]{1,0:T(8,128)S(1)} all-reduce(f32[16,2]{1,0:T(8,128)S(1)} %reshape.742), channel_id=1, replica_groups=mesh['half'=2,'dom'=16,'slab'=8] {'slab'}, use_global_device_ids=true, to_apply=%region_15.16 | all-reduce | flops 32 | bytes 256 | tf_op jit(solution)/shard_map/psum | solution.py:176
  668.4 86.2 %all-reduce.3.cloned.1.call-done = f32[16,2,32,32]{3,2,1,0:T(8,128)} async-done(((f32[16,2,32,32]{3,2,1,0:T(8,128)}), f32[16,2,32,32]{3,2,1,0:T(8,128)}) %all-reduce.3.cloned.1.call-update) | async-done | bytes 131088 | tf_op jit(solution)/shard_map/psum | solution.py:176
  756.5 7.2 all-to-all-start.2
  763.7 3.3 fusion.2
  767.0 2.8 copy.90
  (125 shorter events, 34.4 us)
Async XLA Ops:
  7.2 3.2 copy-start
  7.2 4.2 copy-start.25
  7.2 4.2 copy-start.28
  7.2 14.5 %copy-start.7 = (bf16[1,8,48,384]{3,2,1,0:T(8,128)(2,1)S(1)}, bf16[1,8,48,384]{3,2,1,0:T(8,128)(2,1)}, u32[]{:S(2)}) copy-start(bf16[1,8,48,384]{3,2,1,0:T(8,128)(2,1)} %param.7) | copy-start | bytes 884740
  8.8 56.7 %collective-permute-start = (bf16[32,48,384]{2,0,1:T(8,128)(2,1)S(1)}, bf16[32,48,384]{2,0,1:T(8,128)(2,1)}, u32[]{:S(2)}, u32[]{:S(2)}) collective-permute-start(bf16[32,48,384]{2,0,1:T(8,128)(2,1)S(1)} %bitcast.128), channel_id=1, source_target_pairs={{0,128},{128,0},{1,129},{129,1},{2,130},{130,2},{3,131},{131,3},{4... | collective-permute-start | bytes 3538952 | tf_op jit(solution)/shard_map/ppermute | solution.py:15
  11.5 8.2 %copy-start.27 = (s32[8]{0:T(128)}, s32[8]{0:T(128)S(1)}, u32[]{:S(2)}) copy-start(s32[8]{0:T(128)S(1)} %fusion.104) | copy-start | bytes 100
  12.7 26.9 %all-to-all-start = ((s32[16,2,5]{2,1,0:T(2,128)}), s32[16,2,5]{2,1,0:T(2,128)S(1)}, u32[]{:S(2)}, u32[]{:S(2)}) async-start(s32[16,2,5]{2,1,0:T(2,128)} %bitcast.13), calls=%async_computation | async-start | bytes 32768 | tf_op jit(solution)/shard_map/all_to_all | solution.py:121
  19.7 4.0 copy-start.14
  20.0 3.7 copy-start.22
  20.0 3.7 copy-start.20
  25.6 28.1 %copy-start.2 = (bf16[1,32,48,384]{3,2,1,0:T(8,128)(2,1)S(1)}, bf16[1,32,48,384]{3,2,1,0:T(8,128)(2,1)}, u32[]{:S(2)}) copy-start(bf16[1,32,48,384]{3,2,1,0:T(8,128)(2,1)} %param.13) | copy-start | bytes 3538948
  40.2 22.6 %all-to-all-start.1 = ((bf16[16,2,48,384]{3,1,2,0:T(2,128)(2,1)}), bf16[16,2,48,384]{3,1,2,0:T(2,128)(2,1)S(1)}, u32[]{:S(2)}, u32[]{:S(2)}) async-start(bf16[16,2,48,384]{3,1,2,0:T(2,128)(2,1)} %copy.76), calls=%async_computation.1 | async-start | bytes 2359296 | tf_op jit(solution)/shard_map/all_to_all | solution.py:120
  46.0 708.7 %all-reduce.3.cloned.1.call-start = ((), (), s32[]{:S(2)}) async-start(), calls=%async_computation.3 | async-start | bytes 1048576 | tf_op jit(solution)/shard_map/psum | solution.py:176
  564.2 57.9 %copy-start.15 = (s32[48]{0:T(128)S(1)}, s32[48]{0:T(128)}, u32[]{:S(2)}) copy-start(s32[48]{0:T(128)} %copy-done.14) | copy-start | bytes 580
  564.2 58.6 %copy-start.3 = (f32[32,48,192]{2,1,0:T(8,128)S(1)}, f32[32,48,192]{2,1,0:T(8,128)}, u32[]{:S(2)}) copy-start(f32[32,48,192]{2,1,0:T(8,128)} %get-tuple-element.41) | copy-start | bytes 3538948
  564.2 58.6 %copy-start.8 = (s32[32,192]{1,0:T(8,128)S(1)}, s32[32,192]{1,0:T(8,128)}, u32[]{:S(2)}) copy-start(s32[32,192]{1,0:T(8,128)} %iota_multiply_fusion) | copy-start | bytes 73732
  564.2 58.6 %copy-start.9 = (s32[32,48]{0,1:T(8,128)S(1)}, s32[32,48]{0,1:T(8,128)}, u32[]{:S(2)}) copy-start(s32[32,48]{0,1:T(8,128)} %broadcast_multiply_fusion) | copy-start | bytes 18436
  564.3 58.6 %copy-start.18 = (s32[32]{0:T(128)S(1)}, s32[32]{0:T(128)}, u32[]{:S(2)}) copy-start(s32[32]{0:T(128)} %get-tuple-element.24) | copy-start | bytes 388
  564.3 58.6 %copy-start.19 = (f32[32]{0:T(128)S(1)}, f32[32]{0:T(128)}, u32[]{:S(2)}) copy-start(f32[32]{0:T(128)} %fusion.77) | copy-start | bytes 388
  564.3 58.6 %copy-start.26 = (f32[16]{0:T(128)S(1)}, f32[16]{0:T(128)}, u32[]{:S(2)}) copy-start(f32[16]{0:T(128)} %param.11) | copy-start | bytes 196
  639.1 3.3 copy-start.1
  650.0 113.7 %copy-start.5 = (bf16[32,48,192]{2,0,1:T(8,128)(2,1)S(1)}, bf16[32,48,192]{2,0,1:T(8,128)(2,1)}, u32[]{:S(2)}) copy-start(bf16[32,48,192]{2,0,1:T(8,128)(2,1)} %get-tuple-element.28) | copy-start | bytes 1769476
  756.5 13.3 %all-to-all-start.2 = ((f32[16,1,2]{2,1,0:T(1,128)}), f32[16,1,2]{2,1,0:T(1,128)S(1)}, u32[]{:S(2)}, u32[]{:S(2)}) async-start(f32[16,1,2]{2,1,0:T(1,128)} %bitcast.36), calls=%async_computation.2 | async-start | bytes 16384 | tf_op jit(solution)/shard_map/all_to_all | solution.py:179
  767.0 5.0 copy-start.23
  (10 other events, 16.7 us)
Sparse Core Ops, SparseCore 0:
  650.1 104.5 all-reduce.2
where the time goes:
time: 782 us; the launch traced here: 779 us
  blocking collectives  310 us (40%)
  other arithmetic  218 us (28%)
  waiting for transfers between devices  107 us (14%)
  local copies, waits for them, and re-layouts  83.9 us (11%)
  matrix products  23.9 us (3%)
  starting transfers between devices  21.6 us (3%)
  between operations  14.5 us (2%)
    psum x1, blocking collectives, on_device(): lax.psum((shell_sum(cross_part, shells), shell_sum(first_sq, shells), she...  295 us
    scatter-add x3, other arithmetic, shell_sum(): jax.ops.segment_sum(values.reshape(-1), shells.reshape(-1), num_segments=...  194 us
    psum x1, waiting for transfers between devices, on_device(): corr_total, energy_total = lax.psum((corr_part, energy_part), 'slab')  86.2 us
    gather x2, local copies, waits for them, and re-layouts, on_device(): weight = jnp.take(jnp.maximum(shell_corr, 0.1), shells)  57.8 us
  transfers between devices with their start and end apart: 5, of which 3 were waited for; matrix products, arithmetic and copies ran while one was open for 4% of the time, Pallas kernels for 0%

commit v1 on v0

v1 whole, which is shorter than its diff:
```python
import functools
import math

import jax
import jax.numpy as jnp
import ml_dtypes
import numpy as np
from jax import lax
from jax.experimental import pallas as pl
from jax.experimental.pallas import tpu as pltpu
from jax.sharding import PartitionSpec as P

BOX = 384
KX = 192
SHIFTS = 32
NSHELL = 267
ROWS = 48
SLABS = 8
DOMS = 16
PART = 8
ORI = 32
CLASSES = 16
SLOTS = 32
SHELLS = 384
CHUNK = 4
NCHUNK = 4
F32 = jnp.float32
BF16 = jnp.bfloat16
I32 = jnp.int32
MESH = pl.DeviceIdType.MESH


def tables():
    row = np.arange(BOX)
    ky = np.where(row < KX, row, row - BOX)
    kx = np.arange(KX)
    q = ky[:, None] ** 2 + kx[None, :] ** 2
    radius = np.floor(np.sqrt(q.astype(np.float64))).astype(np.int64)
    radius -= radius * radius > q
    radius += (radius + 1) * (radius + 1) <= q
    shell = np.clip(radius - 1, 0, NSHELL - 1)
    base = np.array([0, 0, 0, 128, 128, 0, 0, 0])
    local = shell.reshape(SLABS, ROWS, KX) - base[:, None, None]
    assert local.min() >= 0 and local.max() < 256
    shell_of = np.concatenate([local, local], axis=-1).astype(np.int32)
    ends = np.zeros((SLABS, ROWS, 256), np.int32)
    for s in range(256):
        ends[:, :, s] = (local <= s).sum(-1)
    freq = np.concatenate([q, q], axis=-1).reshape(SLABS, ROWS, BOX).astype(np.float32)
    freq = freq / np.float32(BOX * BOX)
    unit = np.float32(2.0 * math.pi / BOX)

    def trig(index):
        angle = (np.mod(index, BOX).astype(np.float32) * unit).astype(np.float32)
        return np.cos(angle).astype(np.float32), np.sin(angle).astype(np.float32)

    shift = np.arange(33) - 16
    cx, sx = trig(shift[:, None] * kx[None, :])
    tx = np.zeros((33, 8, BOX), np.float32)
    tx[:, 0] = np.concatenate([cx, cx], -1)
    tx[:, 1] = np.concatenate([sx, sx], -1)
    tx[:, 2] = np.concatenate([cx, -cx], -1)
    tx[:, 3] = np.concatenate([sx, -sx], -1)
    cy, sy = trig(ky[:, None] * shift[None, :])
    ty = np.zeros((SLABS, 2, ROWS, 128), np.float32)
    ty[:, 0, :, :33] = cy.reshape(SLABS, ROWS, 33)
    ty[:, 1, :, :33] = sy.reshape(SLABS, ROWS, 33)

    window = np.arange(SHIFTS) - SHIFTS // 2
    wcx, wsx = trig(kx[:, None] * window[None, :])
    wcy, wsy = trig(ky[:, None] * window[None, :])
    col_re = np.concatenate([wcx, -wsx], axis=0)
    col_im = np.concatenate([wsx, wcx], axis=0)
    col = np.zeros((4 * BOX, 256), np.float32)
    for k in range(4):
        col[k * BOX : (k + 1) * BOX, 32 * k : 32 * k + 32] = col_re
        col[k * BOX : (k + 1) * BOX, 128 + 32 * k : 160 + 32 * k] = col_im
    wcy = wcy.reshape(SLABS, ROWS, SHIFTS).transpose(0, 2, 1)
    wsy = wsy.reshape(SLABS, ROWS, SHIFTS).transpose(0, 2, 1)
    rowt = np.concatenate([wcy, -wsy], axis=-1)
    tri = (np.arange(BOX)[:, None] % KX <= np.arange(256)[None, :]).astype(np.float32)
    bf = ml_dtypes.bfloat16
    return (
        shell_of, ends, freq, tx, ty, col.astype(bf), rowt.astype(bf), tri.astype(bf),
    )


def flip_halves(x):
    return pltpu.roll(x, KX, 1)


def ctf_rows(freq, defocus):
    g = defocus * freq
    phi = math.atan2(0.1, 0.995)
    m = jnp.floor((g + phi) * (1.0 / math.pi) + 0.5)
    t = ((g - m * 3.140625) - m * 9.67653589793e-4) + phi
    odd = m - 2.0 * jnp.floor(m * 0.5)
    t2 = t * t
    p = -1.0 / 39916800.0
    for c in (1.0 / 362880.0, -1.0 / 5040.0, 1.0 / 120.0, -1.0 / 6.0, 1.0):
        p = p * t2 + c
    scale = math.sqrt(0.995 * 0.995 + 0.01)
    return (p * t) * ((2.0 * odd - 1.0) * scale)


def split3(x):
    hi = x.astype(BF16)
    rest = x - hi.astype(F32)
    mid = rest.astype(BF16)
    low = (rest - mid.astype(F32)).astype(BF16)
    return hi, mid, low


def main_kernel(
    ori_ref, off_ref, cls_ref, defocus_ref, slot_ref,
    img_hbm, map_hbm,
    shell_hbm, ends_hbm, freq_hbm, tx_hbm, ty_hbm, col_hbm, rowt_hbm, tri_hbm,
    score_ref, corr_ref, weight_ref, contrib_hbm, ctf_hbm, meta_hbm,
    img, maps, other, shell_of, ends, freq, tx, ty, col, rowt, tri,
    packed, items, contrib, vprod, eprod, ctf, eyb, meta_out, meta_in, meta_own, meta_all,
    ar1, ar2, ar3, arx, prod, part, parts_in, ret, ret_out,
    load_sem, map_send, map_recv, img_send, img_recv, meta_send, meta_recv, own_sem,
    ar1_send, ar1_recv, ar2_send, ar2_recv, ar3_send, ar3_recv,
    part_send, part_recv, ret_send, ret_recv, out_sem,
):
    h = lax.axis_index("half")
    d = lax.axis_index("dom")
    z = lax.axis_index("slab")
    y = d // 4
    q = d % 4

    def remote(src, dst, send, recv, where):
        return pltpu.make_async_remote_copy(
            src_ref=src, dst_ref=dst, send_sem=send, recv_sem=recv,
            device_id=where, device_id_type=MESH,
        )

    loads = [
        (map_hbm, maps), (img_hbm, img), (freq_hbm.at[z], freq), (ty_hbm.at[z], ty),
        (tx_hbm, tx), (tri_hbm, tri), (ends_hbm.at[z], ends), (shell_hbm.at[z], shell_of),
        (col_hbm, col), (rowt_hbm.at[z], rowt),
    ]
    loads = [pltpu.make_async_copy(a, b, load_sem.at[i]) for i, (a, b) in enumerate(loads)]
    for c in loads:
        c.start()
    (ld_map, ld_img, ld_freq, ld_ty, ld_tx, ld_tri, ld_ends, ld_shell, ld_col, ld_rowt) = loads

    barrier = pltpu.get_barrier_semaphore()
    pl.semaphore_signal(barrier, inc=1, device_id={"half": 1 - h}, device_id_type=MESH)
    for r in range(1, DOMS):
        pl.semaphore_signal(barrier, inc=1, device_id={"dom": (d + r) % DOMS}, device_id_type=MESH)
    for r in range(1, 4):
        pl.semaphore_signal(
            barrier, inc=1, device_id={"half": 1 - h, "dom": y * 4 + (q + r) % 4}, device_id_type=MESH
        )
    for r in range(1, SLABS):
        pl.semaphore_signal(barrier, inc=1, device_id={"slab": (z + r) % SLABS}, device_id_type=MESH)

    lane1 = lax.broadcasted_iota(I32, (1, 128), 1)
    owner_row = lax.broadcasted_iota(I32, (DOMS, 128), 0)
    lane16 = lax.broadcasted_iota(I32, (DOMS, 128), 1)
    owners = []
    ranks = []
    message = jnp.zeros((DOMS, 128), I32)
    for p in range(PART):
        place = slot_ref[ori_ref[p]]
        owner = place // ORI
        rank = jnp.int32(0)
        for before in owners:
            rank = rank + jnp.where(before == owner, 1, 0)
        owners.append(owner)
        ranks.append(rank)
        fields = (cls_ref[p], off_ref[p, 0] + 16, off_ref[p, 1] + 16, place % ORI, jnp.int32(1), jnp.int32(p))
        at = lane16 - 8 * rank
        for f, value in enumerate(fields):
            message = jnp.where((owner_row == owner) & (at == f), value, message)
    for o in range(DOMS):
        meta_out[o] = message[o : o + 1]
    own_copy = pltpu.make_async_copy(meta_out, meta_own, own_sem.at[0])
    own_copy.start()

    pl.semaphore_wait(barrier, 1 + (DOMS - 1) + 3 + (SLABS - 1))

    map_copies = []
    for c in range(NCHUNK):
        source = map_hbm.at[pl.ds((1 - h) * (ORI // 2) + c * CHUNK, CHUNK)]
        copy = remote(
            source, other.at[pl.ds(c * CHUNK, CHUNK)], map_send.at[c], map_recv.at[c], {"half": 1 - h}
        )
        copy.start()
        map_copies.append(copy)

    meta_copies = []
    for r in range(1, DOMS):
        o = (d + r) % DOMS
        copy = remote(meta_out.at[o], meta_in.at[d], meta_send.at[r], meta_recv.at[d], {"dom": o})
        copy.start()
        meta_copies.append(copy)
    own_copy.wait()
    ld_img.wait()

    def pack(o, carry):
        for e in range(2):
            packed[o, e] = img[meta_own[o, 0, 8 * e + 5]]
        return carry

    lax.fori_loop(0, DOMS, pack, 0)
    img_copies = []
    for r in range(1, DOMS):
        o = (d + r) % DOMS
        copy = remote(packed.at[o], items.at[d], img_send.at[r], img_recv.at[d], {"dom": o})
        copy.start()
        img_copies.append(copy)
    self_img = pltpu.make_async_copy(packed.at[d], items.at[d], own_sem.at[1])
    self_img.start()
    self_meta = pltpu.make_async_copy(meta_out.at[d], meta_in.at[d], own_sem.at[2])
    self_meta.start()

    ld_freq.wait()

    def one_class(k, carry):
        ctf[k] = ctf_rows(freq[...], defocus_ref[k])
        return carry

    lax.fori_loop(0, CLASSES, one_class, 0)
    ctf_out = pltpu.make_async_copy(ctf, ctf_hbm, out_sem.at[0])
    ctf_out.start()
    ld_ty.wait()
    for part_of in range(2):
        for s in range(33):
            eyb[s, part_of] = jnp.broadcast_to(ty[part_of, :, s : s + 1], (ROWS, 128))

    ld_map.wait()

    def own_power(i, total):
        m = maps[i].astype(F32)
        return total + m * m

    own_sq = lax.fori_loop(0, ORI, own_power, jnp.zeros((ROWS, BOX), F32))
    cross = jnp.zeros((ROWS, BOX), F32)
    for c in range(NCHUNK):
        map_copies[c].wait_recv()

        def cross_term(i, total):
            mine = maps[h * (ORI // 2) + c * CHUNK + i].astype(F32)
            return total + mine * other[c * CHUNK + i].astype(F32)

        cross = lax.fori_loop(0, CHUNK, cross_term, cross)

    ld_tri.wait()
    ld_ends.wait()
    pieces = jnp.concatenate(list(split3(cross)) + list(split3(own_sq)), axis=0)
    running = jnp.dot(pieces, tri[...], preferred_element_type=F32)
    lane = lax.broadcasted_iota(I32, (1, 128), 1)
    sums = []
    for v in range(2):
        o = 3 * ROWS * v
        c = running[o : o + ROWS] + (running[o + ROWS : o + 2 * ROWS] + running[o + 2 * ROWS : o + 3 * ROWS])
        blocks = []
        for b in range(2):
            e = ends[:, 128 * b : 128 * b + 128]
            low = jnp.take_along_axis(c[:, :128], jnp.clip(e - 1, 0, 127), axis=1)
            high = jnp.take_along_axis(c[:, 128:], jnp.clip(e - 129, 0, 127), axis=1)
            got = jnp.where(e > 128, high, jnp.where(e > 0, low, 0.0))
            blocks.append(jnp.sum(got, axis=0, keepdims=True))
        first = blocks[0] - jnp.where(lane == 0, 0.0, pltpu.roll(blocks[0], 1, 1))
        carry_in = jnp.where(lane == 0, blocks[0][:, 127:128], pltpu.roll(blocks[1], 1, 1))
        sums.append((first, blocks[1] - carry_in))
    shifted = (z == 3) | (z == 4)
    sub = lax.broadcasted_iota(I32, (8, 128), 0)
    for b in range(3):
        rows = []
        for v in range(2):
            s0, s1 = sums[v]
            zero = jnp.zeros((1, 128), F32)
            plain = (s0, s1, zero)[b]
            moved = (zero, s0, s1)[b]
            rows.append(jnp.where(shifted, moved, plain))
        block = jnp.where(sub == 0, rows[0], jnp.where(sub == 1 + h, rows[1], 0.0))
        arx[0, :, 128 * b : 128 * b + 128] = block

    g = h * 4 + q
    ar1_copies = []
    for r in range(1, 8):
        to = (g + r) % 8
        copy = remote(
            arx.at[0], ar1.at[g], ar1_send.at[r], ar1_recv.at[g], {"half": to // 4, "dom": y * 4 + to % 4}
        )
        copy.start()
        ar1_copies.append(copy)

    for r in range(1, DOMS):
        s = (d + r) % DOMS
        remote(meta_out.at[s], meta_in.at[s], meta_send.at[r], meta_recv.at[s], {"dom": s}).wait_recv()
    self_meta.wait()
    to_smem = pltpu.make_async_copy(meta_in, meta_all, own_sem.at[3])
    to_smem.start()
    meta_save = pltpu.make_async_copy(meta_in, meta_hbm, out_sem.at[1])
    meta_save.start()
    ld_tx.wait()
    for r in range(1, DOMS):
        s = (d + r) % DOMS
        remote(packed.at[s], items.at[s], img_send.at[r], img_recv.at[s], {"dom": s}).wait_recv()
    self_img.wait()
    to_smem.wait()
    low_half = lax.broadcasted_iota(I32, (ROWS, BOX), 1) < KX

    def one_item(n, carry):
        b = n // 2
        at = 8 * (n % 2)
        phase_x = tx[meta_all[b, 0, at + 1]]
        phase_y = eyb[meta_all[b, 0, at + 2]]
        cy = jnp.concatenate([phase_y[0]] * 3, axis=1)
        sy = jnp.concatenate([phase_y[1]] * 3, axis=1)
        cos_t = phase_x[0:1] * cy - phase_x[1:2] * sy
        sin_t = phase_x[3:4] * cy + phase_x[2:3] * sy
        x = items[b, n % 2].astype(F32)
        c = ctf[meta_all[b, 0, at]] * meta_all[b, 0, at + 4].astype(F32)
        zz = c * (x * cos_t + flip_halves(x) * sin_t)
        contrib[n] = zz.astype(BF16)
        m = maps[meta_all[b, 0, at + 3]].astype(F32)
        straight = zz * m
        crossed = zz * flip_halves(m)
        vprod[n] = jnp.where(low_half, straight, -crossed) + flip_halves(
            jnp.where(low_half, crossed, straight)
        )
        cm = c * m
        eprod[n] = cm * cm
        return carry

    lax.fori_loop(0, 12, one_item, 0)
    total = arx[0]
    for r in range(1, 8):
        s = (g + r) % 8
        remote(
            arx.at[0], ar1.at[s], ar1_send.at[r], ar1_recv.at[s], {"half": s // 4, "dom": y * 4 + s % 4}
        ).wait_recv()
        total = total + ar1[s]
    arx[1] = total
    ar2_copies = []
    for r in range(1, 4):
        to = (y + r) % 4
        copy = remote(arx.at[1], ar2.at[y], ar2_send.at[r], ar2_recv.at[y], {"dom": to * 4 + q})
        copy.start()
        ar2_copies.append(copy)
    lax.fori_loop(12, 22, one_item, 0)
    for r in range(1, 4):
        s = (y + r) % 4
        remote(arx.at[1], ar2.at[s], ar2_send.at[r], ar2_recv.at[s], {"dom": s * 4 + q}).wait_recv()
        total = total + ar2[s]
    arx[2] = total
    ar3_copies = []
    for r in range(1, SLABS):
        to = (z + r) % SLABS
        copy = remote(arx.at[2], ar3.at[z], ar3_send.at[r], ar3_recv.at[z], {"slab": to})
        copy.start()
        ar3_copies.append(copy)
    lax.fori_loop(22, SLOTS, one_item, 0)
    contrib_out = pltpu.make_async_copy(contrib, contrib_hbm, out_sem.at[2])
    contrib_out.start()
    ar3[z] = total
    for r in range(1, SLABS):
        s = (z + r) % SLABS
        remote(arx.at[2], ar3.at[s], ar3_send.at[r], ar3_recv.at[s], {"slab": s}).wait_recv()
    total = ar3[0]
    for s in range(1, SLABS):
        total = total + ar3[s]

    fsc = total[0:1] / jnp.sqrt(total[1:2] * total[2:3] + 1e-06)
    corr_ref[...] = fsc
    floor = jnp.maximum(fsc, 0.1)
    table0 = jnp.where(shifted, floor[:, 128:256], floor[:, 0:128])
    table1 = jnp.where(shifted, floor[:, 256:384], floor[:, 128:256])
    table0 = jnp.broadcast_to(table0, (ROWS, 128))
    table1 = jnp.broadcast_to(table1, (ROWS, 128))
    ld_shell.wait()
    for b in range(3):
        at = shell_of[:, 128 * b : 128 * b + 128]
        low = jnp.take_along_axis(table0, jnp.minimum(at, 127), axis=1)
        high = jnp.take_along_axis(table1, jnp.maximum(at - 128, 0), axis=1)
        weight_ref[:, 128 * b : 128 * b + 128] = jnp.where(at < 128, low, high)
    w = weight_ref[...]

    def weigh(t, carry):
        for k in range(4):
            prod[t, :, BOX * k : BOX * k + BOX] = (vprod[4 * t + k] * w).astype(BF16)
            e = jnp.sum(eprod[4 * t + k] * w, axis=0, keepdims=True)
            part[t, 32 + k : 33 + k, :] = e[:, 0:128] + e[:, 128:256] + e[:, 256:384]
        return carry

    lax.fori_loop(0, SLABS, weigh, 0)
    ld_col.wait()
    ld_rowt.wait()
    section = jnp.dot(
        prod[...].reshape(SLABS * ROWS, 4 * BOX), col[...], preferred_element_type=F32
    ).astype(BF16)
    stacked = jnp.concatenate(
        [
            jnp.concatenate(
                [section[ROWS * t : ROWS * t + ROWS, :128], section[ROWS * t : ROWS * t + ROWS, 128:]], axis=0
            )
            for t in range(SLABS)
        ],
        axis=1,
    )
    partial = jnp.dot(rowt[...], stacked, preferred_element_type=F32)
    for t in range(SLABS):
        part[t, 0:32, :] = partial[:, 128 * t : 128 * t + 128]

    part_copies = []
    for r in range(1, SLABS):
        to = (z + r) % SLABS
        copy = remote(part.at[to], parts_in.at[z], part_send.at[r], part_recv.at[z], {"slab": to})
        copy.start()
        part_copies.append(copy)
    whole = part[z]
    for r in range(1, SLABS):
        s = (z + r) % SLABS
        remote(part.at[s], parts_in.at[s], part_send.at[r], part_recv.at[s], {"slab": s}).wait_recv()
        whole = whole + parts_in[s]
    best = jnp.max(whole[0:32], axis=0, keepdims=True)
    answer = jnp.zeros((1, 128), F32)
    for k in range(4):
        top = jnp.max(jnp.where(lane1 // 32 == k, best, -jnp.inf), axis=1, keepdims=True)
        energy = jnp.sum(whole[32 + k : 33 + k], axis=1, keepdims=True)
        answer = jnp.where(lane1 == k, top / jnp.sqrt(energy + 1e-06), answer)
    ret_out[...] = answer

    for e in range(2):
        for r in range(SLABS):
            holder = 2 * z + e
            to = (z + r) % SLABS
            copy = remote(
                ret_out, ret.at[d], ret_send.at[8 * e + r], ret_recv.at[d], {"dom": holder, "slab": to}
            )
            if r == 0:
                pl.when(holder != d)(copy.start)
            else:
                copy.start()

    @pl.when(d // 2 == z)
    def _():
        ret[d] = answer

    for r in range(DOMS):
        s = (d + r) % DOMS
        copy = remote(ret_out, ret.at[s], ret_send.at[r], ret_recv.at[s], {"dom": s, "slab": d // 2})
        if r == 0:
            pl.when(d // 2 != z)(copy.wait_recv)
        else:
            copy.wait_recv()
    scores = jnp.zeros((1, 128), F32)
    for p in range(PART):
        row = ret[owners[p]]
        value = jnp.sum(jnp.where(lane1 == 2 * (d % 2) + ranks[p], row, 0.0), axis=1, keepdims=True)
        scores = jnp.where(lane1 == p, value, scores)
    score_ref[...] = scores[:, :PART]

    for copy in map_copies + meta_copies + img_copies + ar1_copies + ar2_copies + ar3_copies + part_copies:
        copy.wait_send()
    for e in range(2):
        for r in range(SLABS):
            holder = 2 * z + e
            to = (z + r) % SLABS
            copy = remote(
                ret_out, ret.at[d], ret_send.at[8 * e + r], ret_recv.at[d], {"dom": holder, "slab": to}
            )
            if r == 0:
                pl.when(holder != d)(copy.wait_send)
            else:
                copy.wait_send()
    ctf_out.wait()
    meta_save.wait()
    contrib_out.wait()


def run_main(orientation, offsets, classes, defocus, slots, images, maps, consts):
    smem = pl.BlockSpec(memory_space=pltpu.SMEM)
    hbm = pl.BlockSpec(memory_space=pl.ANY)
    vmem = pl.BlockSpec(memory_space=pltpu.VMEM)
    v = pltpu.VMEM
    dma = pltpu.SemaphoreType.DMA
    return pl.pallas_call(
        main_kernel,
        out_shape=(
            jax.ShapeDtypeStruct((1, PART), F32),
            jax.ShapeDtypeStruct((1, SHELLS), F32),
            jax.ShapeDtypeStruct((ROWS, BOX), F32),
            jax.ShapeDtypeStruct((SLOTS, ROWS, BOX), BF16),
            jax.ShapeDtypeStruct((CLASSES, ROWS, BOX), F32),
            jax.ShapeDtypeStruct((DOMS, 1, 128), I32),
        ),
        in_specs=[smem] * 5 + [hbm] * 10,
        out_specs=(vmem, vmem, vmem, hbm, hbm, hbm),
        scratch_shapes=[
            v((PART, ROWS, BOX), BF16),
            v((ORI, ROWS, BOX), BF16),
            v((ORI // 2, ROWS, BOX), BF16),
            v((ROWS, BOX), I32),
            v((ROWS, 256), I32),
            v((ROWS, BOX), F32),
            v((33, 8, BOX), F32),
            v((2, ROWS, 128), F32),
            v((4 * BOX, 256), BF16),
            v((SHIFTS, 2 * ROWS), BF16),
            v((BOX, 256), BF16),
            v((DOMS, 2, ROWS, BOX), BF16),
            v((DOMS, 2, ROWS, BOX), BF16),
            v((SLOTS, ROWS, BOX), BF16),
            v((SLOTS, ROWS, BOX), F32),
            v((SLOTS, ROWS, BOX), F32),
            v((CLASSES, ROWS, BOX), F32),
            v((33, 2, ROWS, 128), F32),
            v((DOMS, 1, 128), I32),
            v((DOMS, 1, 128), I32),
            pltpu.SMEM((DOMS, 1, 128), I32),
            pltpu.SMEM((DOMS, 1, 128), I32),
            v((8, 8, SHELLS), F32),
            v((4, 8, SHELLS), F32),
            v((8, 8, SHELLS), F32),
            v((3, 8, SHELLS), F32),
            v((SLABS, ROWS, 4 * BOX), BF16),
            v((SLABS, 40, 128), F32),
            v((SLABS, 40, 128), F32),
            v((DOMS, 1, 128), F32),
            v((1, 128), F32),
            dma((10,)),
            dma((NCHUNK,)), dma((NCHUNK,)),
            dma((DOMS,)), dma((DOMS,)),
            dma((DOMS,)), dma((DOMS,)),
            dma((4,)),
            dma((8,)), dma((8,)),
            dma((4,)), dma((4,)),
            dma((8,)), dma((8,)),
            dma((8,)), dma((8,)),
            dma((16,)), dma((16,)),
            dma((3,)),
        ],
        compiler_params=pltpu.CompilerParams(
            collective_id=0, has_side_effects=True, vmem_limit_bytes=48 * 1024 * 1024
        ),
        name="refine",
    )(orientation, offsets, classes, defocus, slots, images, maps, *consts)


STRIP = 16


def maps_kernel(meta, contrib, maps, ctf, weight, out, bottom):
    w = weight[...]
    inverse = 1.0 / w

    def init(r, carry):
        out[r] = maps[r].astype(F32) * inverse
        bottom[r] = inverse
        return carry

    lax.fori_loop(0, ORI, init, 0)

    def add(n, carry):
        b = n // 2
        at = 8 * (n % 2)

        @pl.when(meta[b, at + 4] != 0)
        def _():
            row = meta[b, at + 3]
            c = ctf[meta[b, at]]
            out[row] += contrib[n].astype(F32)
            bottom[row] += c * c

        return carry

    lax.fori_loop(0, SLOTS, add, 0)

    def finish(r, carry):
        out[r] = out[r] / bottom[r]
        return carry

    lax.fori_loop(0, ORI, finish, 0)


def run_maps(meta, contrib, maps, ctf, weight):
    def block(count):
        return pl.BlockSpec((count, STRIP, BOX), lambda i: (0, i, 0))

    return pl.pallas_call(
        maps_kernel,
        grid=(ROWS // STRIP,),
        out_shape=jax.ShapeDtypeStruct((ORI, ROWS, BOX), F32),
        in_specs=[
            pl.BlockSpec(memory_space=pltpu.SMEM),
            block(SLOTS), block(ORI), block(CLASSES),
            pl.BlockSpec((STRIP, BOX), lambda i: (i, 0)),
        ],
        out_specs=block(ORI),
        scratch_shapes=[pltpu.VMEM((ORI, STRIP, BOX), F32)],
        compiler_params=pltpu.CompilerParams(vmem_limit_bytes=32 * 1024 * 1024),
        name="new_maps",
    )(meta, contrib, maps, ctf, weight)


def on_device(consts, images, orientation, offsets, defocus_class, defocus, ori_slot, half_maps):
    scores, fsc, weight, contrib, ctf, meta = run_main(
        orientation[0], offsets[0], defocus_class[0], defocus, ori_slot, images[0], half_maps[0], consts
    )
    new_maps = run_maps(meta[:, 0], contrib, half_maps[0], ctf, weight)
    return scores, new_maps[None], fsc[0, :NSHELL]


def solution(mesh):
    in_specs = (
        P("half", "dom", "slab", None),
        P("half", "dom"),
        P("half", "dom", None),
        P("half", "dom"),
        P(),
        P(),
        P("half", "dom", "slab", None),
    )
    out_specs = (P("half", "dom"), P("half", "dom", "slab", None), P())
    return jax.shard_map(
        functools.partial(on_device, tables()),
        mesh=mesh, in_specs=in_specs, out_specs=out_specs, check_vma=False,
    )
```

time: 782 us -> 87.5 us (0.11)
  blocking collectives: 310 us -> 0 us
  other arithmetic: 218 us -> 0 us
  waiting for transfers between devices: 107 us -> 0 us
  Pallas kernels: 0 us -> 72.8 us
  local copies, waits for them, and re-layouts: 83.9 us -> 13.5 us
  matrix products: 23.9 us -> 0 us
  starting transfers between devices: 21.6 us -> 0 us
  between operations: 14.5 us -> 0.66 us
    psum x2 -> x0, blocking collectives: 310 us -> none  [the longest x1 295 us: on_device(): lax.psum((shell_sum(cross_part, shells), shell_sum(first_sq, shells), she...]
    scatter-add x3 -> x0, other arithmetic: 194 us -> none  [shell_sum(): jax.ops.segment_sum(values.reshape(-1), shells.reshape(-1), num_segments=...]
    psum x1 -> x0, waiting for transfers between devices: 86.2 us -> none  [on_device(): corr_total, energy_total = lax.psum((corr_part, energy_part), 'slab')]
    pallas_call x0 -> x2, Pallas kernels: none -> 72.8 us  [the longest x1 66.9 us: run_main(): pl.pallas_call(main_kernel, out_shape=(jax.ShapeDtypeStruct((1, PART), F3...]
    gather x4 -> x0, local copies, waits for them, and re-layouts: 59.2 us -> none  [the longest x2 57.8 us: on_device(): weight = jnp.take(jnp.maximum(shell_corr, 0.1), shells)]
    dot_general x7 -> x0, matrix products: 23.9 us -> none  [the longest x1 13.6 us: on_device(): jnp.dot(class_hot, ctf.reshape(classes, -1), precision=lax.Precision.HIGH...]
    all_to_all x3 -> x0, waiting for transfers between devices: 21.2 us -> none  [the longest x1 14 us: on_device(): lax.all_to_all(packed_meta, 'dom', split_axis=0, concat_axis=0, tiled=True)]
    all_to_all x3 -> x0, starting transfers between devices: 20 us -> none  [the longest x1 7.24 us: on_device(): lax.all_to_all(slot_score, 'dom', split_axis=0, concat_axis=0, tiled=True)]
  transfers between devices with their start and end apart: 5 -> 0, of which waited for: 3 -> 0; matrix products, arithmetic and copies ran while one was open for 4% -> 0% of each run, Pallas kernels for 0% -> 0%
where the time goes in v1:
time: 87.5 us; the launch traced here: 87 us
  Pallas kernels  72.8 us (83%)
  local copies, waits for them, and re-layouts  13.5 us (15%)
    pallas_call x1, Pallas kernels, run_main(): pl.pallas_call(main_kernel, out_shape=(jax.ShapeDtypeStruct((1, PART), F3...  66.9 us
    unnamed x29, local copies, waits for them, and re-layouts  12.1 us
    pallas_call x1, Pallas kernels, run_maps(): pl.pallas_call(maps_kernel, grid=(ROWS // STRIP,), out_shape=jax.ShapeDty...  5.89 us

profile of v1, /device:TPU:16, one launch (start us, length us, event | category | flops | bytes accessed | tf_op | source)
XLA Modules:
  0.0 87.0 jit_solution(4231436558740611552)
XLA Ops:
  0.6 0.8 copy.18.off_ref
  1.4 0.0 copy-start.1
  1.4 1.1 %copy-done.1 = bf16[1536,256]{1,0:T(8,128)(2,1)S(1)} copy-done((bf16[1536,256]{1,0:T(8,128)(2,1)S(1)}, bf16[1536,256]{1,0:T(8,128)(2,1)}, u32[]{:S(2)}) %copy-start.1) | copy-done | bytes 786456
  2.5 0.0 copy-start.2
  2.5 1.1 %copy-done.2 = f32[8,48,384]{2,1,0:T(8,128)S(1)} copy-done((f32[8,48,384]{2,1,0:T(8,128)S(1)}, f32[8,48,384]{2,1,0:T(8,128)}, u32[]{:S(2)}) %copy-start.2) | copy-done | bytes 589848
  3.6 0.0 copy-start.3
  3.6 1.1 %copy-done.3 = s32[8,48,384]{2,1,0:T(8,128)S(1)} copy-done((s32[8,48,384]{2,1,0:T(8,128)S(1)}, s32[8,48,384]{2,1,0:T(8,128)}, u32[]{:S(2)}) %copy-start.3) | copy-done | bytes 589848
  4.6 0.0 copy-start.4
  4.6 1.0 %copy-done.4 = f32[33,8,384]{2,1,0:T(8,128)S(1)} copy-done((f32[33,8,384]{2,1,0:T(8,128)S(1)}, f32[33,8,384]{2,1,0:T(8,128)}, u32[]{:S(2)}) %copy-start.4) | copy-done | bytes 405528
  5.6 0.0 copy-start.5
  5.7 1.0 %copy-done.5 = f32[8,2,48,128]{3,2,1,0:T(8,128)S(1)} copy-done((f32[8,2,48,128]{3,2,1,0:T(8,128)S(1)}, f32[8,2,48,128]{3,2,1,0:T(8,128)}, u32[]{:S(2)}) %copy-start.5) | copy-done | bytes 393240
  6.6 1.0 %copy-done.6 = s32[8,48,256]{2,1,0:T(8,128)S(1)} copy-done((s32[8,48,256]{2,1,0:T(8,128)S(1)}, s32[8,48,256]{2,1,0:T(8,128)}, u32[]{:S(2)}) %copy-start.6) | copy-done | bytes 393240
  7.6 1.0 %copy-done.7 = bf16[1,8,48,384]{3,2,1,0:T(8,128)(2,1)S(1)} copy-done((bf16[1,8,48,384]{3,2,1,0:T(8,128)(2,1)S(1)}, bf16[1,8,48,384]{3,2,1,0:T(8,128)(2,1)}, u32[]{:S(2)}) %copy-start.7) | copy-done | bytes 294936
  8.6 0.9 %copy-done.8 = bf16[384,256]{1,0:T(8,128)(2,1)S(1)} copy-done((bf16[384,256]{1,0:T(8,128)(2,1)S(1)}, bf16[384,256]{1,0:T(8,128)(2,1)}, u32[]{:S(2)}) %copy-start.8) | copy-done | bytes 196632
  9.5 0.8 copy-done.9
  10.4 0.7 copy-done.10
  11.1 0.7 copy-done.11
  11.7 0.7 copy-done.12
  12.4 0.7 copy-done.13
  13.0 66.9 %refine.1 = (f32[1,8]{1,0:T(1,128)S(1)}, f32[1,384]{1,0:T(1,128)S(1)}, f32[48,384]{1,0:T(8,128)S(1)}, bf16[32,48,384]{2,1,0:T(8,128)(2,1)S(1)}, f32[16,48,384]{2,1,0:T(8,128)S(1)}, /*index=5*/s32[16,1,128]{2,1,0:T(1,128)S(1)}) custom-call(s32[8]{0:T(128)S(1)} %bitcast.11, s32[8,2]{1,0:T(8,128)S(1)} %copy.18.off_ref, s32[8]{0:T(128)S(1)} %bitcast.12, ...), custom_call_target="tpu_custom_call" | custom-call | tf_op jit(solution)/shard_map/refine/pallas_call | solution.py:483
  80.0 0.0 copy-done
  80.0 5.9 %new_maps.1 = f32[32,48,384]{2,1,0:T(8,128)} custom-call(s32[16,128]{1,0:T(8,128)S(1)} %bitcast.10, bf16[32,48,384]{2,1,0:T(8,128)(2,1)S(1)} %get-tuple-element.11.contrib, bf16[32,48,384]{2,1,0:T(8,128)(2,1)S(1)} %bitcast.8, f32[16,48,384]{2,1,0:T(8,128)S(1)} %get-tuple-element.12.ctf, f32[48,384]{1,0:T(8,128)S(1)} %get-tuple-element.13.weight), custom_call_target="tpu_custom_call" | custom-call | tf_op jit(solution)/shard_map/new_maps/pallas_call | solution.py:586
  85.9 0.6 slice_reduce_fusion
  86.5 0.5 copy.20
  (9 shorter events, 0.0 us)
Async XLA Ops:
  1.4 1.1 %copy-start.1 = (bf16[1536,256]{1,0:T(8,128)(2,1)S(1)}, bf16[1536,256]{1,0:T(8,128)(2,1)}, u32[]{:S(2)}) copy-start(bf16[1536,256]{1,0:T(8,128)(2,1)} %constant.21.clone.col_hbm) | copy-start | bytes 2359300
  2.5 1.1 %copy-start.2 = (f32[8,48,384]{2,1,0:T(8,128)S(1)}, f32[8,48,384]{2,1,0:T(8,128)}, u32[]{:S(2)}) copy-start(f32[8,48,384]{2,1,0:T(8,128)} %constant.18.clone.freq_hbm) | copy-start | bytes 1769476
  3.6 1.1 %copy-start.3 = (s32[8,48,384]{2,1,0:T(8,128)S(1)}, s32[8,48,384]{2,1,0:T(8,128)}, u32[]{:S(2)}) copy-start(s32[8,48,384]{2,1,0:T(8,128)} %constant.16.clone.shell_hbm) | copy-start | bytes 1769476
  4.6 1.0 %copy-start.4 = (f32[33,8,384]{2,1,0:T(8,128)S(1)}, f32[33,8,384]{2,1,0:T(8,128)}, u32[]{:S(2)}) copy-start(f32[33,8,384]{2,1,0:T(8,128)} %constant.19.clone.tx_hbm) | copy-start | bytes 1216516
  5.6 1.0 %copy-start.5 = (f32[8,2,48,128]{3,2,1,0:T(8,128)S(1)}, f32[8,2,48,128]{3,2,1,0:T(8,128)}, u32[]{:S(2)}) copy-start(f32[8,2,48,128]{3,2,1,0:T(8,128)} %constant.20.clone.ty_hbm) | copy-start | bytes 1179652
  6.6 1.0 %copy-start.6 = (s32[8,48,256]{2,1,0:T(8,128)S(1)}, s32[8,48,256]{2,1,0:T(8,128)}, u32[]{:S(2)}) copy-start(s32[8,48,256]{2,1,0:T(8,128)} %constant.17.clone.ends_hbm) | copy-start | bytes 1179652
  7.6 1.0 %copy-start.7 = (bf16[1,8,48,384]{3,2,1,0:T(8,128)(2,1)S(1)}, bf16[1,8,48,384]{3,2,1,0:T(8,128)(2,1)}, u32[]{:S(2)}) copy-start(bf16[1,8,48,384]{3,2,1,0:T(8,128)(2,1)} %param.15) | copy-start | bytes 884740
  8.6 0.9 %copy-start.8 = (bf16[384,256]{1,0:T(8,128)(2,1)S(1)}, bf16[384,256]{1,0:T(8,128)(2,1)}, u32[]{:S(2)}) copy-start(bf16[384,256]{1,0:T(8,128)(2,1)} %constant.23.clone.tri_hbm) | copy-start | bytes 589828
  9.5 0.8 copy-start.9
  10.4 0.7 copy-start.10
  11.1 0.7 copy-start.11
  11.7 0.7 copy-start.12
  12.4 0.7 copy-start.13
  13.0 66.9 %copy-start = (bf16[1,32,48,384]{3,2,1,0:T(8,128)(2,1)S(1)}, bf16[1,32,48,384]{3,2,1,0:T(8,128)(2,1)}, u32[]{:S(2)}) copy-start(bf16[1,32,48,384]{3,2,1,0:T(8,128)(2,1)} %param.21) | copy-start | bytes 3538948

commit v2 on v1

v2 whole, which is shorter than its diff:
```python
import functools
import math

import jax
import jax.numpy as jnp
import ml_dtypes
import numpy as np
from jax import lax
from jax.experimental import pallas as pl
from jax.experimental.pallas import tpu as pltpu
from jax.sharding import PartitionSpec as P

BOX = 384
KX = 192
SHIFTS = 32
NSHELL = 267
ROWS = 48
SLABS = 8
DOMS = 16
PART = 8
ORI = 32
CLASSES = 16
SLOTS = 32
SHELLS = 384
CHUNK = 4
NCHUNK = 4
F32 = jnp.float32
BF16 = jnp.bfloat16
I32 = jnp.int32
MESH = pl.DeviceIdType.MESH
FAR8 = (4, 3, 5, 2, 6, 1, 7)
NEAR8 = FAR8[::-1]
FAR4 = (2, 1, 3)
NEAR4 = FAR4[::-1]


def tables():
    row = np.arange(BOX)
    ky = np.where(row < KX, row, row - BOX)
    kx = np.arange(KX)
    q = ky[:, None] ** 2 + kx[None, :] ** 2
    radius = np.floor(np.sqrt(q.astype(np.float64))).astype(np.int64)
    radius -= radius * radius > q
    radius += (radius + 1) * (radius + 1) <= q
    shell = np.clip(radius - 1, 0, NSHELL - 1)
    base = np.array([0, 0, 0, 128, 128, 0, 0, 0])
    local = shell.reshape(SLABS, ROWS, KX) - base[:, None, None]
    assert local.min() >= 0 and local.max() < 256
    shell_of = np.concatenate([local, local], axis=-1).astype(np.int32)
    ends = np.zeros((SLABS, ROWS, 256), np.int32)
    for s in range(256):
        ends[:, :, s] = (local <= s).sum(-1)
    freq = np.concatenate([q, q], axis=-1).reshape(SLABS, ROWS, BOX).astype(np.float32)
    freq = freq / np.float32(BOX * BOX)
    unit = np.float32(2.0 * math.pi / BOX)

    def trig(index):
        angle = (np.mod(index, BOX).astype(np.float32) * unit).astype(np.float32)
        return np.cos(angle).astype(np.float32), np.sin(angle).astype(np.float32)

    shift = np.arange(33) - 16
    cx, sx = trig(shift[:, None] * kx[None, :])
    tx = np.zeros((33, 8, BOX), np.float32)
    tx[:, 0] = np.concatenate([cx, cx], -1)
    tx[:, 1] = np.concatenate([sx, sx], -1)
    tx[:, 2] = np.concatenate([cx, -cx], -1)
    tx[:, 3] = np.concatenate([sx, -sx], -1)
    cy, sy = trig(ky[:, None] * shift[None, :])
    ty = np.zeros((SLABS, 2, ROWS, 128), np.float32)
    ty[:, 0, :, :33] = cy.reshape(SLABS, ROWS, 33)
    ty[:, 1, :, :33] = sy.reshape(SLABS, ROWS, 33)

    window = np.arange(SHIFTS) - SHIFTS // 2
    wcx, wsx = trig(kx[:, None] * window[None, :])
    wcy, wsy = trig(ky[:, None] * window[None, :])
    col_re = np.concatenate([wcx, -wsx], axis=0)
    col_im = np.concatenate([wsx, wcx], axis=0)
    col = np.zeros((4 * BOX, 256), np.float32)
    for k in range(4):
        col[k * BOX : (k + 1) * BOX, 32 * k : 32 * k + 32] = col_re
        col[k * BOX : (k + 1) * BOX, 128 + 32 * k : 160 + 32 * k] = col_im
    wcy = wcy.reshape(SLABS, ROWS, SHIFTS).transpose(0, 2, 1)
    wsy = wsy.reshape(SLABS, ROWS, SHIFTS).transpose(0, 2, 1)
    rowt = np.concatenate([wcy, -wsy], axis=-1)
    tri = (np.arange(BOX)[:, None] % KX <= np.arange(256)[None, :]).astype(np.float32)
    bf = ml_dtypes.bfloat16
    return (
        shell_of, ends, freq, tx, ty, col.astype(bf), rowt.astype(bf), tri.astype(bf),
    )


def flip_halves(x):
    return pltpu.roll(x, KX, 1)


def ctf_rows(freq, defocus):
    g = defocus * freq
    phi = math.atan2(0.1, 0.995)
    m = jnp.floor((g + phi) * (1.0 / math.pi) + 0.5)
    t = ((g - m * 3.140625) - m * 9.67653589793e-4) + phi
    odd = m - 2.0 * jnp.floor(m * 0.5)
    t2 = t * t
    p = -1.0 / 39916800.0
    for c in (1.0 / 362880.0, -1.0 / 5040.0, 1.0 / 120.0, -1.0 / 6.0, 1.0):
        p = p * t2 + c
    scale = math.sqrt(0.995 * 0.995 + 0.01)
    return (p * t) * ((2.0 * odd - 1.0) * scale)


def split3(x):
    hi = x.astype(BF16)
    rest = x - hi.astype(F32)
    mid = rest.astype(BF16)
    low = (rest - mid.astype(F32)).astype(BF16)
    return hi, mid, low


def main_kernel(
    ori_hbm, off_hbm, cls_hbm, defocus_hbm, slot_hbm, img_hbm, map_hbm,
    shell_hbm, ends_hbm, freq_hbm, tx_hbm, ty_hbm, col_hbm, rowt_hbm, tri_hbm,
    score_ref, corr_ref, new_ref,
    ori_ref, off_ref, cls_ref, defocus_ref, slot_ref,
    img, maps, other, shell_of, ends, freq, tx, ty, col, rowt, tri, weight_ref,
    packed, stage, regular, extra, contrib, vprod, eprod, ctf, eyb,
    meta_out, meta_stage, meta_in, meta_own, meta_all, link_v, link,
    ar1, ar2, ar3, arx, prod, part, parts_in, ret, ret_out,
    load_sem, own_sem, ring_sem, map_send, map_recv,
    img1_send, img1_recv, img2_send, img2_recv, ext_send, ext_recv,
    meta1_send, meta1_recv, meta2_send, meta2_recv,
    ar1_send, ar1_recv, ar2_send, ar2_recv, ar3_send, ar3_recv,
    part_send, part_recv, ret_send, ret_recv,
):
    h = lax.axis_index("half")
    d = lax.axis_index("dom")
    z = lax.axis_index("slab")
    y = d // 4
    q = d % 4
    g = h * 4 + q

    def flip(bits):
        hi = (q // 2 + bits // 2) % 2
        lo = (q % 2 + bits % 2) % 2
        return hi * 2 + lo

    def remote(src, dst, send, recv, where):
        return pltpu.make_async_remote_copy(
            src_ref=src, dst_ref=dst, send_sem=send, recv_sem=recv,
            device_id=where, device_id_type=MESH,
        )

    def signal(sem, where):
        pl.semaphore_signal(sem, inc=1, device_id=where, device_id_type=MESH)

    barrier = pltpu.get_barrier_semaphore()
    for r in FAR8:
        to = (g + r) % 8
        signal(barrier, {"half": to // 4, "dom": y * 4 + to % 4})
    for r in FAR4:
        signal(barrier, {"dom": (y + r) % 4 * 4 + q})
    for r in (1, SLABS - 1):
        signal(barrier, {"slab": (z + r) % SLABS})

    loads = [
        (ori_hbm, ori_ref), (off_hbm, off_ref), (cls_hbm, cls_ref), (slot_hbm, slot_ref),
        (defocus_hbm, defocus_ref), (img_hbm, img), (freq_hbm.at[z], freq), (ty_hbm.at[z], ty),
        (map_hbm, maps), (tri_hbm, tri), (ends_hbm.at[z], ends), (tx_hbm, tx),
        (shell_hbm.at[z], shell_of), (col_hbm, col), (rowt_hbm.at[z], rowt),
    ]
    loads = [pltpu.make_async_copy(a, b, load_sem.at[i]) for i, (a, b) in enumerate(loads)]
    for c in loads:
        c.start()
    ld_small = loads[:4]
    (ld_defocus, ld_img, ld_freq, ld_ty, ld_map, ld_tri, ld_ends, ld_tx, ld_shell, ld_col, ld_rowt) = loads[4:]

    for c in ld_small:
        c.wait()
    lane1 = lax.broadcasted_iota(I32, (1, 128), 1)
    owner_row = lax.broadcasted_iota(I32, (DOMS, 128), 0)
    lane16 = lax.broadcasted_iota(I32, (DOMS, 128), 1)
    owners = []
    ranks = []
    second = jnp.int32(0)
    message = jnp.zeros((DOMS, 128), I32)
    for p in range(PART):
        place = slot_ref[ori_ref[p]]
        owner = place // ORI
        rank = jnp.int32(0)
        for before in owners:
            rank = rank + jnp.where(before == owner, 1, 0)
        owners.append(owner)
        ranks.append(rank)
        second = jnp.where(rank == 1, p, second)
        fields = (cls_ref[p], off_ref[0, p] + 16, off_ref[1, p] + 16, place % ORI, jnp.int32(1), jnp.int32(p))
        at = lane16 - 8 * rank
        for f, value in enumerate(fields):
            message = jnp.where((owner_row == owner) & (at == f), value, message)
    for o in range(DOMS):
        meta_out[o // 4, o % 4] = message[o : o + 1]
    own_copy = pltpu.make_async_copy(meta_out, meta_own, own_sem.at[0])
    own_copy.start()

    pl.semaphore_wait(barrier, 7 + 3 + 2)

    map_copies = []
    for c in range(NCHUNK):
        source = map_hbm.at[pl.ds((1 - h) * (ORI // 2) + c * CHUNK, CHUNK)]
        copy = remote(
            source, other.at[pl.ds(c * CHUNK, CHUNK)], map_send.at[c], map_recv.at[c], {"half": 1 - h}
        )
        copy.start()
        map_copies.append(copy)
    copies = list(map_copies)

    def ring(k):
        for r in (1, SLABS - 1):
            signal(ring_sem.at[k], {"slab": (z + r) % SLABS})

    ring(0)

    for r in FAR4:
        to = (y + r) % 4
        copy = remote(
            meta_out.at[to], meta_stage.at[:, y], meta1_send.at[r], meta1_recv.at[y], {"dom": to * 4 + q}
        )
        copy.start()
        copies.append(copy)
    own_copy.wait()
    ld_img.wait()

    def pack(o, carry):
        packed[o // 4, o % 4] = img[meta_own[o // 4, o % 4, 0, 5]]
        return carry

    lax.fori_loop(0, DOMS, pack, 0)
    for t in range(4):
        packed[t, 4] = img[second]
    for r in FAR4:
        to = (y + r) % 4
        copy = remote(packed.at[to], stage.at[:, y], img1_send.at[r], img1_recv.at[y], {"dom": to * 4 + q})
        copy.start()
        copies.append(copy)
    own_img = pltpu.make_async_copy(packed.at[y], stage.at[:, y], own_sem.at[1])
    own_img.start()
    own_meta = pltpu.make_async_copy(meta_out.at[y], meta_stage.at[:, y], own_sem.at[2])
    own_meta.start()
    pl.semaphore_wait(ring_sem.at[0], 2)
    ring(1)

    ld_freq.wait()
    ld_defocus.wait()

    def one_class(k, carry):
        ctf[k] = ctf_rows(freq[...], defocus_ref[k])
        return carry

    lax.fori_loop(0, CLASSES, one_class, 0)
    pl.semaphore_wait(ring_sem.at[1], 2)
    ring(2)
    ld_ty.wait()
    for part_of in range(2):
        for s in range(33):
            eyb[s, part_of] = jnp.broadcast_to(ty[part_of, :, s : s + 1], (ROWS, 128))

    for r in FAR4:
        s = (y + r) % 4
        remote(meta_out.at[s], meta_stage.at[:, s], meta1_send.at[r], meta1_recv.at[s], {"dom": s * 4 + q}).wait_recv()
    own_meta.wait()
    for bits in (3, 2, 1):
        to = flip(bits)
        copy = remote(
            meta_stage.at[to], meta_in.at[q], meta2_send.at[bits], meta2_recv.at[q], {"dom": y * 4 + to}
        )
        copy.start()
        copies.append(copy)
    last_meta = pltpu.make_async_copy(meta_stage.at[q], meta_in.at[q], own_sem.at[3])
    last_meta.start()

    ld_map.wait()

    def own_power(i, total):
        m = maps[i].astype(F32)
        return total + m * m

    own_sq = lax.fori_loop(0, ORI, own_power, jnp.zeros((ROWS, BOX), F32))
    pl.semaphore_wait(ring_sem.at[2], 2)
    cross = jnp.zeros((ROWS, BOX), F32)
    for c in range(NCHUNK):
        if c == NCHUNK - 1:
            for r in FAR4:
                s = (y + r) % 4
                remote(
                    packed.at[s], stage.at[:, s], img1_send.at[r], img1_recv.at[s], {"dom": s * 4 + q}
                ).wait_recv()
            own_img.wait()
            for kind, (src, dst, send, recv) in enumerate(
                ((stage.at[4], extra, ext_send, ext_recv), (stage.at[flip(1)], regular, img2_send, img2_recv))
            ):
                copy = remote(src, dst.at[q], send.at[1], recv.at[q], {"dom": y * 4 + flip(1)})
                copy.start()
                copies.append(copy)
            own_regular = pltpu.make_async_copy(stage.at[q], regular.at[q], own_sem.at[4])
            own_regular.start()
            own_extra = pltpu.make_async_copy(stage.at[4], extra.at[q], own_sem.at[5])
            own_extra.start()
        map_copies[c].wait_recv()

        def cross_term(i, total):
            mine = maps[h * (ORI // 2) + c * CHUNK + i].astype(F32)
            return total + mine * other[c * CHUNK + i].astype(F32)

        cross = lax.fori_loop(0, CHUNK, cross_term, cross)

    copy = remote(stage.at[4], extra.at[q], ext_send.at[2], ext_recv.at[q], {"dom": y * 4 + flip(2)})
    copy.start()
    copies.append(copy)
    for bits in (2, 3):
        to = flip(bits)
        copy = remote(stage.at[to], regular.at[q], img2_send.at[bits], img2_recv.at[q], {"dom": y * 4 + to})
        copy.start()
        copies.append(copy)

    ld_tri.wait()
    ld_ends.wait()
    pieces = jnp.concatenate(list(split3(cross)) + list(split3(own_sq)), axis=0)
    running = jnp.dot(pieces, tri[...], preferred_element_type=F32)
    lane = lax.broadcasted_iota(I32, (1, 128), 1)
    sums = []
    for v in range(2):
        o = 3 * ROWS * v
        c = running[o : o + ROWS] + (running[o + ROWS : o + 2 * ROWS] + running[o + 2 * ROWS : o + 3 * ROWS])
        blocks = []
        for b in range(2):
            e = ends[:, 128 * b : 128 * b + 128]
            low = jnp.take_along_axis(c[:, :128], jnp.clip(e - 1, 0, 127), axis=1)
            high = jnp.take_along_axis(c[:, 128:], jnp.clip(e - 129, 0, 127), axis=1)
            got = jnp.where(e > 128, high, jnp.where(e > 0, low, 0.0))
            blocks.append(jnp.sum(got, axis=0, keepdims=True))
        first = blocks[0] - jnp.where(lane == 0, 0.0, pltpu.roll(blocks[0], 1, 1))
        carry_in = jnp.where(lane == 0, blocks[0][:, 127:128], pltpu.roll(blocks[1], 1, 1))
        sums.append((first, blocks[1] - carry_in))
    shifted = (z == 3) | (z == 4)
    sub = lax.broadcasted_iota(I32, (8, 128), 0)
    for b in range(3):
        rows = []
        for v in range(2):
            s0, s1 = sums[v]
            zero = jnp.zeros((1, 128), F32)
            plain = (s0, s1, zero)[b]
            moved = (zero, s0, s1)[b]
            rows.append(jnp.where(shifted, moved, plain))
        block = jnp.where(sub == 0, rows[0], jnp.where(sub == 1 + h, rows[1], 0.0))
        arx[0, :, 128 * b : 128 * b + 128] = block

    for r in FAR8:
        to = (g + r) % 8
        copy = remote(
            arx.at[0], ar1.at[g], ar1_send.at[r], ar1_recv.at[g], {"half": to // 4, "dom": y * 4 + to % 4}
        )
        copy.start()
        copies.append(copy)

    last_meta.wait()
    for bits in (1, 2, 3):
        s = flip(bits)
        remote(meta_stage.at[s], meta_in.at[s], meta2_send.at[bits], meta2_recv.at[s], {"dom": y * 4 + s}).wait_recv()
    to_smem = pltpu.make_async_copy(meta_in, meta_all, own_sem.at[6])
    to_smem.start()

    numbers = jnp.concatenate([meta_in[c, t] for c in range(4) for t in range(4)], axis=0).astype(F32)

    def field(f):
        return jnp.sum(jnp.where(lane16 == f, numbers, 0.0), axis=1, keepdims=True)

    key = jnp.concatenate(
        [jnp.where(field(8 * e + 4) > 0.5, field(8 * e + 3), -1.0) for e in range(2)], axis=0
    )
    item_lane = lax.broadcasted_iota(I32, (SLOTS, 128), 1)
    item_row = lax.broadcasted_iota(I32, (SLOTS, 128), 0)
    across = jnp.sum(jnp.where(item_lane == item_row, key, 0.0), axis=0, keepdims=True)
    where_f = item_lane.astype(F32)
    last = jnp.max(
        jnp.where((across == item_row.astype(F32)) & (item_lane < SLOTS), where_f, -1.0), axis=1, keepdims=True
    )
    same = (across == key) & (item_lane < item_row) & (key >= 0.0)
    previous = jnp.max(jnp.where(same, where_f, -1.0), axis=1, keepdims=True)
    link_v[...] = jnp.where(item_lane == 0, last, jnp.where(item_lane == 1, previous, 0.0)).astype(I32)
    link_copy = pltpu.make_async_copy(link_v, link, own_sem.at[7])
    link_copy.start()

    ld_tx.wait()
    own_regular.wait()
    own_extra.wait()
    to_smem.wait()
    low_half = lax.broadcasted_iota(I32, (ROWS, BOX), 1) < KX

    def items_of(source, column, e):
        def one_item(t, carry):
            at = 8 * e
            phase_x = tx[meta_all[column, t, 0, at + 1]]
            phase_y = eyb[meta_all[column, t, 0, at + 2]]
            cy = jnp.concatenate([phase_y[0]] * 3, axis=1)
            sy = jnp.concatenate([phase_y[1]] * 3, axis=1)
            cos_t = phase_x[0:1] * cy - phase_x[1:2] * sy
            sin_t = phase_x[3:4] * cy + phase_x[2:3] * sy
            x = source[column, t].astype(F32)
            c = ctf[meta_all[column, t, 0, at]] * meta_all[column, t, 0, at + 4].astype(F32)
            zz = c * (x * cos_t + flip_halves(x) * sin_t)
            contrib[16 * e + 4 * column + t] = zz.astype(BF16)
            m = maps[meta_all[column, t, 0, at + 3]].astype(F32)
            straight = zz * m
            crossed = zz * flip_halves(m)
            n = 2 * (4 * t + column) + e
            vprod[n] = jnp.where(low_half, straight, -crossed) + flip_halves(
                jnp.where(low_half, crossed, straight)
            )
            cm = c * m
            eprod[n] = cm * cm
            return carry

        lax.fori_loop(0, 4, one_item, 0)

    def wait_regular(bits):
        s = flip(bits)
        remote(
            stage.at[s], regular.at[s], img2_send.at[bits], img2_recv.at[s], {"dom": y * 4 + s}
        ).wait_recv()

    def wait_extra(bits):
        s = flip(bits)
        remote(stage.at[4], extra.at[s], ext_send.at[bits], ext_recv.at[s], {"dom": y * 4 + s}).wait_recv()

    items_of(regular, q, 0)
    items_of(extra, q, 1)
    total = arx[0]
    for r in NEAR8:
        s = (g + r) % 8
        remote(
            arx.at[0], ar1.at[s], ar1_send.at[r], ar1_recv.at[s], {"half": s // 4, "dom": y * 4 + s % 4}
        ).wait_recv()
        total = total + ar1[s]
    arx[1] = total
    for r in FAR4:
        to = (y + r) % 4
        copy = remote(arx.at[1], ar2.at[y], ar2_send.at[r], ar2_recv.at[y], {"dom": to * 4 + q})
        copy.start()
        copies.append(copy)
    wait_extra(1)
    items_of(extra, flip(1), 1)
    wait_regular(1)
    items_of(regular, flip(1), 0)
    for r in NEAR4:
        s = (y + r) % 4
        remote(arx.at[1], ar2.at[s], ar2_send.at[r], ar2_recv.at[s], {"dom": s * 4 + q}).wait_recv()
        total = total + ar2[s]
    arx[2] = total
    for r in FAR8:
        to = (z + r) % SLABS
        copy = remote(arx.at[2], ar3.at[z], ar3_send.at[r], ar3_recv.at[z], {"slab": to})
        copy.start()
        copies.append(copy)
    wait_extra(2)
    copy = remote(
        extra.at[flip(2)], extra.at[flip(2)], ext_send.at[3], ext_recv.at[flip(2)], {"dom": y * 4 + flip(1)}
    )
    copy.start()
    copies.append(copy)
    items_of(extra, flip(2), 1)
    wait_regular(2)
    items_of(regular, flip(2), 0)
    wait_extra(3)
    items_of(extra, flip(3), 1)
    wait_regular(3)
    items_of(regular, flip(3), 0)
    ar3[z] = total
    for r in NEAR8:
        s = (z + r) % SLABS
        remote(arx.at[2], ar3.at[s], ar3_send.at[r], ar3_recv.at[s], {"slab": s}).wait_recv()
    total = ar3[0]
    for s in range(1, SLABS):
        total = total + ar3[s]

    fsc = total[0:1] / jnp.sqrt(total[1:2] * total[2:3] + 1e-06)
    corr_ref[...] = fsc
    floor = jnp.maximum(fsc, 0.1)
    table0 = jnp.where(shifted, floor[:, 128:256], floor[:, 0:128])
    table1 = jnp.where(shifted, floor[:, 256:384], floor[:, 128:256])
    table0 = jnp.broadcast_to(table0, (ROWS, 128))
    table1 = jnp.broadcast_to(table1, (ROWS, 128))
    ld_shell.wait()
    for b in range(3):
        at = shell_of[:, 128 * b : 128 * b + 128]
        low = jnp.take_along_axis(table0, jnp.minimum(at, 127), axis=1)
        high = jnp.take_along_axis(table1, jnp.maximum(at - 128, 0), axis=1)
        weight_ref[:, 128 * b : 128 * b + 128] = jnp.where(at < 128, low, high)
    w = weight_ref[...]

    def weigh(t, carry):
        for k in range(4):
            prod[t, :, BOX * k : BOX * k + BOX] = (vprod[4 * t + k] * w).astype(BF16)
            e = jnp.sum(eprod[4 * t + k] * w, axis=0, keepdims=True)
            part[t, 32 + k : 33 + k, :] = e[:, 0:128] + e[:, 128:256] + e[:, 256:384]
        return carry

    lax.fori_loop(0, SLABS, weigh, 0)
    ld_col.wait()
    ld_rowt.wait()
    section = jnp.dot(
        prod[...].reshape(SLABS * ROWS, 4 * BOX), col[...], preferred_element_type=F32
    ).astype(BF16)
    stacked = jnp.concatenate(
        [
            jnp.concatenate(
                [section[ROWS * t : ROWS * t + ROWS, :128], section[ROWS * t : ROWS * t + ROWS, 128:]], axis=0
            )
            for t in range(SLABS)
        ],
        axis=1,
    )
    partial = jnp.dot(rowt[...], stacked, preferred_element_type=F32)
    for t in range(SLABS):
        part[t, 0:32, :] = partial[:, 128 * t : 128 * t + 128]

    for r in FAR8:
        to = (z + r) % SLABS
        copy = remote(part.at[to], parts_in.at[z], part_send.at[r], part_recv.at[z], {"slab": to})
        copy.start()
        copies.append(copy)

    link_copy.wait()

    def add_item(u, carry):
        e = u // 16
        before = link[u, 1]
        has = jnp.where(before >= 0, 1.0, 0.0)
        from_u = jnp.minimum(jnp.maximum(before, 0), SLOTS - 1)
        column = (u % 16) // 4
        t = u % 4
        c = ctf[meta_all[column, t, 0, 8 * e]]
        valid = meta_all[column, t, 0, 8 * e + 4].astype(F32)
        vprod[u] = contrib[u].astype(F32) + has * vprod[from_u]
        eprod[u] = (c * c) * valid + has * eprod[from_u]
        return carry

    lax.fori_loop(0, SLOTS, add_item, 0)
    whole = part[z]
    for r in NEAR8:
        s = (z + r) % SLABS
        remote(part.at[s], parts_in.at[s], part_send.at[r], part_recv.at[s], {"slab": s}).wait_recv()
        whole = whole + parts_in[s]
    best = jnp.max(whole[0:32], axis=0, keepdims=True)
    answer = jnp.zeros((1, 128), F32)
    for k in range(4):
        top = jnp.max(jnp.where(lane1 // 32 == k, best, -jnp.inf), axis=1, keepdims=True)
        energy = jnp.sum(whole[32 + k : 33 + k], axis=1, keepdims=True)
        answer = jnp.where(lane1 == k, top / jnp.sqrt(energy + 1e-06), answer)
    ret_out[...] = answer

    def score_copy(e, r):
        return remote(
            ret_out, ret.at[d], ret_send.at[8 * e + r], ret_recv.at[d],
            {"dom": 2 * z + e, "slab": (z + r) % SLABS},
        )

    for r in FAR8:
        for e in range(2):
            score_copy(e, r).start()
    for e in range(2):
        pl.when(2 * z + e != d)(score_copy(e, 0).start)

    @pl.when(d // 2 == z)
    def _():
        ret[d] = answer

    def one_slice(r, carry):
        at = link[r, 0]
        has = jnp.where(at >= 0, 1.0, 0.0)
        at = jnp.minimum(jnp.maximum(at, 0), SLOTS - 1)
        inverse = 1.0 / weight_ref[...]
        top = has * vprod[at] + maps[r].astype(F32) * inverse
        new_ref[r] = top / (has * eprod[at] + inverse)
        return carry

    lax.fori_loop(0, ORI, one_slice, 0)

    for r in range(DOMS):
        s = (d + r) % DOMS
        copy = remote(ret_out, ret.at[s], ret_send.at[r], ret_recv.at[s], {"dom": s, "slab": d // 2})
        if r == 0:
            pl.when(d // 2 != z)(copy.wait_recv)
        else:
            copy.wait_recv()
    scores = jnp.zeros((1, 128), F32)
    for p in range(PART):
        row = ret[owners[p]]
        value = jnp.sum(jnp.where(lane1 == 2 * (d % 2) + ranks[p], row, 0.0), axis=1, keepdims=True)
        scores = jnp.where(lane1 == p, value, scores)
    score_ref[...] = scores[:, :PART]

    for copy in copies:
        copy.wait_send()
    for e in range(2):
        for r in FAR8:
            score_copy(e, r).wait_send()
        pl.when(2 * z + e != d)(score_copy(e, 0).wait_send)


def run_main(*operands):
    hbm = pl.BlockSpec(memory_space=pltpu.HBM)
    vmem = pl.BlockSpec(memory_space=pltpu.VMEM)
    v = pltpu.VMEM
    smem = pltpu.SMEM
    dma = pltpu.SemaphoreType.DMA
    return pl.pallas_call(
        main_kernel,
        out_shape=(
            jax.ShapeDtypeStruct((1, PART), F32),
            jax.ShapeDtypeStruct((1, SHELLS), F32),
            jax.ShapeDtypeStruct((ORI, ROWS, BOX), F32),
        ),
        in_specs=[hbm] * 15,
        out_specs=(vmem, vmem, vmem),
        scratch_shapes=[
            smem((PART,), I32), smem((2, PART), I32), smem((PART,), I32), smem((CLASSES,), F32),
            smem((512,), I32),
            v((PART, ROWS, BOX), BF16),
            v((ORI, ROWS, BOX), BF16),
            v((ORI // 2, ROWS, BOX), BF16),
            v((ROWS, BOX), I32),
            v((ROWS, 256), I32),
            v((ROWS, BOX), F32),
            v((33, 8, BOX), F32),
            v((2, ROWS, 128), F32),
            v((4 * BOX, 256), BF16),
            v((SHIFTS, 2 * ROWS), BF16),
            v((BOX, 256), BF16),
            v((ROWS, BOX), F32),
            v((4, 5, ROWS, BOX), BF16),
            v((5, 4, ROWS, BOX), BF16),
            v((4, 4, ROWS, BOX), BF16),
            v((4, 4, ROWS, BOX), BF16),
            v((SLOTS, ROWS, BOX), BF16),
            v((SLOTS, ROWS, BOX), F32),
            v((SLOTS, ROWS, BOX), F32),
            v((CLASSES, ROWS, BOX), F32),
            v((33, 2, ROWS, 128), F32),
            v((4, 4, 1, 128), I32),
            v((4, 4, 1, 128), I32),
            v((4, 4, 1, 128), I32),
            smem((4, 4, 1, 128), I32),
            smem((4, 4, 1, 128), I32),
            v((SLOTS, 128), I32),
            smem((SLOTS, 128), I32),
            v((8, 8, SHELLS), F32),
            v((4, 8, SHELLS), F32),
            v((8, 8, SHELLS), F32),
            v((3, 8, SHELLS), F32),
            v((SLABS, ROWS, 4 * BOX), BF16),
            v((SLABS, 40, 128), F32),
            v((SLABS, 40, 128), F32),
            v((DOMS, 1, 128), F32),
            v((1, 128), F32),
            dma((15,)),
            dma((8,)),
            pltpu.SemaphoreType.REGULAR((3,)),
            dma((NCHUNK,)), dma((NCHUNK,)),
            dma((4,)), dma((4,)),
            dma((4,)), dma((4,)),
            dma((4,)), dma((4,)),
            dma((4,)), dma((4,)),
            dma((4,)), dma((4,)),
            dma((8,)), dma((8,)),
            dma((4,)), dma((4,)),
            dma((8,)), dma((8,)),
            dma((8,)), dma((8,)),
            dma((16,)), dma((16,)),
        ],
        compiler_params=pltpu.CompilerParams(
            collective_id=0, has_side_effects=True, vmem_limit_bytes=60 * 1024 * 1024
        ),
        name="refine",
    )(*operands)


def on_device(consts, images, orientation, offsets, defocus_class, defocus, ori_slot, half_maps):
    scores, fsc, new_maps = run_main(
        orientation[0], offsets[0].T, defocus_class[0], defocus, ori_slot, images[0], half_maps[0], *consts
    )
    return scores, new_maps[None], fsc[0, :NSHELL]


def solution(mesh):
    in_specs = (
        P("half", "dom", "slab", None),
        P("half", "dom"),
        P("half", "dom", None),
        P("half", "dom"),
        P(),
        P(),
        P("half", "dom", "slab", None),
    )
    out_specs = (P("half", "dom"), P("half", "dom", "slab", None), P())
    return jax.shard_map(
        functools.partial(on_device, tables()),
        mesh=mesh, in_specs=in_specs, out_specs=out_specs, check_vma=False,
    )
```

time: 87.5 us -> 65.7 us (0.75)
  Pallas kernels: 72.8 us -> 59.4 us
  local copies, waits for them, and re-layouts: 13.5 us -> 5.54 us
    unnamed x29 -> x2, local copies, waits for them, and re-layouts: 12.1 us -> 4.34 us
    pallas_call x1, Pallas kernels: 66.9 us -> 59.4 us  [run_main(): pl.pallas_call(main_kernel, out_shape=(jax.ShapeDtypeStruct((1, PART), F3...]
    pallas_call x1 -> x0, Pallas kernels: 5.89 us -> none  [run_maps(): pl.pallas_call(maps_kernel, grid=(ROWS // STRIP,), out_shape=jax.ShapeDty...]
where the time goes in v2:
time: 65.7 us; the launch traced here: 65.5 us
  Pallas kernels  59.4 us (90%)
  local copies, waits for them, and re-layouts  5.54 us (8%)
    pallas_call x1, Pallas kernels, run_main(): pl.pallas_call(main_kernel, out_shape=(jax.ShapeDtypeStruct((1, PART), F3...  59.4 us
    unnamed x2, local copies, waits for them, and re-layouts  4.34 us

profile of v2, /device:TPU:16, one launch (start us, length us, event | category | flops | bytes accessed | tf_op | source)
XLA Modules:
  0.0 65.5 jit_solution(2944811988280629237)
XLA Ops:
  0.6 59.4 %refine.1 = (f32[1,8]{1,0:T(1,128)}, f32[1,384]{1,0:T(1,128)}, f32[32,48,384]{2,1,0:T(8,128)}) custom-call(s32[8]{0:T(128)} %bitcast.12, s32[2,8]{1,0:T(2,128)} %bitcast.11, s32[8]{0:T(128)} %bitcast.13, f32[16]{0:T(128)} %defocus_hbm.1, s32[512]{0:T(512)} %slot_hbm.1, bf16[8,48,384]{2,1,0:T(8,128)(2,1)} %bitcast.10, bf16[32,48,384]{2,1,0:T(8,128)(2,1)} %bitcast.9, ...), custom_call_target="tpu_custom_call" | custom-call | tf_op jit(solution)/shard_map/refine/pallas_call | solution.py:613
  60.0 1.2 %slice_reduce_fusion = f32[267]{0:T(512)} fusion(f32[1,384]{1,0:T(1,128)} %get-tuple-element.8), kind=kLoop, calls=%fused_computation | loop fusion | bytes 2136 | tf_op jit(solution)/shard_map/slice | solution.py:688
  61.2 1.1 %copy.20 = f32[1,8]{1,0:T(1,128)} copy(f32[1,8]{1,0:T(1,128)} %get-tuple-element.12) | data formatting | bytes 64
  62.3 3.2 %copy.21 = f32[1,32,48,384]{3,2,1,0:T(8,128)} copy(f32[1,32,48,384]{3,2,1,0:T(8,128)} %bitcast.8) | data formatting | bytes 4718592

commit v3 on v2

--- a/solution.py
+++ b/solution.py
@@ -118,17 +118,17 @@
 def main_kernel(
     ori_hbm, off_hbm, cls_hbm, defocus_hbm, slot_hbm, img_hbm, map_hbm,
     shell_hbm, ends_hbm, freq_hbm, tx_hbm, ty_hbm, col_hbm, rowt_hbm, tri_hbm,
-    score_ref, corr_ref, new_ref,
+    score_ref, corr_ref, new_hbm,
     ori_ref, off_ref, cls_ref, defocus_ref, slot_ref,
     img, maps, other, shell_of, ends, freq, tx, ty, col, rowt, tri, weight_ref,
     packed, stage, regular, extra, contrib, vprod, eprod, ctf, eyb,
     meta_out, meta_stage, meta_in, meta_own, meta_all, link_v, link,
-    ar1, ar2, ar3, arx, prod, part, parts_in, ret, ret_out,
+    new_ref, ar1, ar2, ar3, arx, prod, part, parts_in, ret, ret_out,
     load_sem, own_sem, ring_sem, map_send, map_recv,
     img1_send, img1_recv, img2_send, img2_recv, ext_send, ext_recv,
     meta1_send, meta1_recv, meta2_send, meta2_recv,
     ar1_send, ar1_recv, ar2_send, ar2_recv, ar3_send, ar3_recv,
-    part_send, part_recv, ret_send, ret_recv,
+    part_send, part_recv, ret_send, ret_recv, new_sem,
 ):
     h = lax.axis_index("half")
     d = lax.axis_index("dom")
@@ -339,23 +339,18 @@
         carry_in = jnp.where(lane == 0, blocks[0][:, 127:128], pltpu.roll(blocks[1], 1, 1))
         sums.append((first, blocks[1] - carry_in))
     shifted = (z == 3) | (z == 4)
-    sub = lax.broadcasted_iota(I32, (8, 128), 0)
-    for b in range(3):
-        rows = []
-        for v in range(2):
-            s0, s1 = sums[v]
-            zero = jnp.zeros((1, 128), F32)
-            plain = (s0, s1, zero)[b]
-            moved = (zero, s0, s1)[b]
-            rows.append(jnp.where(shifted, moved, plain))
-        block = jnp.where(sub == 0, rows[0], jnp.where(sub == 1 + h, rows[1], 0.0))
-        arx[0, :, 128 * b : 128 * b + 128] = block
+    zero = jnp.zeros((1, 128), F32)
+    for v in range(3):
+        s0, s1 = sums[min(v, 1)]
+        for b in range(3):
+            block = jnp.where(shifted, (zero, s0, s1)[b], (s0, s1, zero)[b])
+            if v > 0:
+                block = jnp.where(h == v - 1, block, zero)
+            arx[0, :, SHELLS * v + 128 * b : SHELLS * v + 128 * b + 128] = block
 
     for r in FAR8:
-        to = (g + r) % 8
-        copy = remote(
-            arx.at[0], ar1.at[g], ar1_send.at[r], ar1_recv.at[g], {"half": to // 4, "dom": y * 4 + to % 4}
-        )
+        to = (z + r) % SLABS
+        copy = remote(arx.at[0], ar1.at[z], ar1_send.at[r], ar1_recv.at[z], {"slab": to})
         copy.start()
         copies.append(copy)
 
@@ -431,12 +426,14 @@
 
     items_of(regular, q, 0)
     items_of(extra, q, 1)
-    total = arx[0]
+    wait_extra(1)
+    items_of(extra, flip(1), 1)
+    ar1[z] = arx[0]
     for r in NEAR8:
-        s = (g + r) % 8
-        remote(
-            arx.at[0], ar1.at[s], ar1_send.at[r], ar1_recv.at[s], {"half": s // 4, "dom": y * 4 + s % 4}
-        ).wait_recv()
+        s = (z + r) % SLABS
+        remote(arx.at[0], ar1.at[s], ar1_send.at[r], ar1_recv.at[s], {"slab": s}).wait_recv()
+    total = ar1[0]
+    for s in range(1, SLABS):
         total = total + ar1[s]
     arx[1] = total
     for r in FAR4:
@@ -444,26 +441,29 @@
         copy = remote(arx.at[1], ar2.at[y], ar2_send.at[r], ar2_recv.at[y], {"dom": to * 4 + q})
         copy.start()
         copies.append(copy)
-    wait_extra(1)
-    items_of(extra, flip(1), 1)
     wait_regular(1)
     items_of(regular, flip(1), 0)
-    for r in NEAR4:
-        s = (y + r) % 4
-        remote(arx.at[1], ar2.at[s], ar2_send.at[r], ar2_recv.at[s], {"dom": s * 4 + q}).wait_recv()
-        total = total + ar2[s]
-    arx[2] = total
-    for r in FAR8:
-        to = (z + r) % SLABS
-        copy = remote(arx.at[2], ar3.at[z], ar3_send.at[r], ar3_recv.at[z], {"slab": to})
-        copy.start()
-        copies.append(copy)
     wait_extra(2)
     copy = remote(
         extra.at[flip(2)], extra.at[flip(2)], ext_send.at[3], ext_recv.at[flip(2)], {"dom": y * 4 + flip(1)}
     )
     copy.start()
     copies.append(copy)
+    ar2[y] = total
+    for r in NEAR4:
+        s = (y + r) % 4
+        remote(arx.at[1], ar2.at[s], ar2_send.at[r], ar2_recv.at[s], {"dom": s * 4 + q}).wait_recv()
+    total = ar2[0]
+    for s in range(1, 4):
+        total = total + ar2[s]
+    arx[2] = total
+    for r in FAR8:
+        to = (g + r) % 8
+        copy = remote(
+            arx.at[2], ar3.at[g], ar3_send.at[r], ar3_recv.at[g], {"half": to // 4, "dom": y * 4 + to % 4}
+        )
+        copy.start()
+        copies.append(copy)
     items_of(extra, flip(2), 1)
     wait_regular(2)
     items_of(regular, flip(2), 0)
@@ -471,15 +471,18 @@
     items_of(extra, flip(3), 1)
     wait_regular(3)
     items_of(regular, flip(3), 0)
-    ar3[z] = total
+    ar3[g] = total
     for r in NEAR8:
-        s = (z + r) % SLABS
-        remote(arx.at[2], ar3.at[s], ar3_send.at[r], ar3_recv.at[s], {"slab": s}).wait_recv()
+        s = (g + r) % 8
+        remote(
+            arx.at[2], ar3.at[s], ar3_send.at[r], ar3_recv.at[s], {"half": s // 4, "dom": y * 4 + s % 4}
+        ).wait_recv()
     total = ar3[0]
-    for s in range(1, SLABS):
+    for s in range(1, 8):
         total = total + ar3[s]
 
-    fsc = total[0:1] / jnp.sqrt(total[1:2] * total[2:3] + 1e-06)
+    power = total[:, SHELLS : 2 * SHELLS] * total[:, 2 * SHELLS : 3 * SHELLS]
+    fsc = total[:, :SHELLS] / jnp.sqrt(power + 1e-06)
     corr_ref[...] = fsc
     floor = jnp.maximum(fsc, 0.1)
     table0 = jnp.where(shifted, floor[:, 128:256], floor[:, 0:128])
@@ -495,10 +498,13 @@
     w = weight_ref[...]
 
     def weigh(t, carry):
+        energies = []
         for k in range(4):
             prod[t, :, BOX * k : BOX * k + BOX] = (vprod[4 * t + k] * w).astype(BF16)
             e = jnp.sum(eprod[4 * t + k] * w, axis=0, keepdims=True)
-            part[t, 32 + k : 33 + k, :] = e[:, 0:128] + e[:, 128:256] + e[:, 256:384]
+            energies.append(e[:, 0:128] + e[:, 128:256] + e[:, 256:384])
+        energies = jnp.concatenate(energies, axis=0)
+        part[t, 32:48, :] = jnp.concatenate(list(split3(energies)) + [jnp.zeros((4, 128), BF16)], axis=0)
         return carry
 
     lax.fori_loop(0, SLABS, weigh, 0)
@@ -518,7 +524,7 @@
     )
     partial = jnp.dot(rowt[...], stacked, preferred_element_type=F32)
     for t in range(SLABS):
-        part[t, 0:32, :] = partial[:, 128 * t : 128 * t + 128]
+        part[t, 0:32, :] = partial[:, 128 * t : 128 * t + 128].astype(BF16)
 
     for r in FAR8:
         to = (z + r) % SLABS
@@ -542,16 +548,17 @@
         return carry
 
     lax.fori_loop(0, SLOTS, add_item, 0)
-    whole = part[z]
+    whole = part[z].astype(F32)
     for r in NEAR8:
         s = (z + r) % SLABS
         remote(part.at[s], parts_in.at[s], part_send.at[r], part_recv.at[s], {"slab": s}).wait_recv()
-        whole = whole + parts_in[s]
+        whole = whole + parts_in[s].astype(F32)
     best = jnp.max(whole[0:32], axis=0, keepdims=True)
     answer = jnp.zeros((1, 128), F32)
     for k in range(4):
         top = jnp.max(jnp.where(lane1 // 32 == k, best, -jnp.inf), axis=1, keepdims=True)
-        energy = jnp.sum(whole[32 + k : 33 + k], axis=1, keepdims=True)
+        energy = whole[32 + k : 33 + k] + (whole[36 + k : 37 + k] + whole[40 + k : 41 + k])
+        energy = jnp.sum(energy, axis=1, keepdims=True)
         answer = jnp.where(lane1 == k, top / jnp.sqrt(energy + 1e-06), answer)
     ret_out[...] = answer
 
@@ -580,7 +587,13 @@
         new_ref[r] = top / (has * eprod[at] + inverse)
         return carry
 
-    lax.fori_loop(0, ORI, one_slice, 0)
+    new_copies = []
+    for t in range(4):
+        lax.fori_loop(8 * t, 8 * t + 8, one_slice, 0)
+        block = pl.ds(8 * t, 8)
+        copy = pltpu.make_async_copy(new_ref.at[block], new_hbm.at[block], new_sem.at[t])
+        copy.start()
+        new_copies.append(copy)
 
     for r in range(DOMS):
         s = (d + r) % DOMS
@@ -602,6 +615,43 @@
         for r in FAR8:
             score_copy(e, r).wait_send()
         pl.when(2 * z + e != d)(score_copy(e, 0).wait_send)
+    for copy in new_copies:
+        copy.wait()
+
+
+DELIVER = 8
+
+
+def deliver_kernel(score_in, corr_in, new_in, score_out, corr_out, new_out, sem):
+    step = ORI // DELIVER
+    copies = []
+    for t in range(DELIVER):
+        block = pl.ds(step * t, step)
+        copies.append(pltpu.make_async_copy(new_in.at[block], new_out.at[block], sem.at[t]))
+    for copy in copies:
+        copy.start()
+    score_out[...] = score_in[...]
+    corr_out[...] = corr_in[0, :NSHELL]
+    for copy in copies:
+        copy.wait()
+
+
+def deliver(scores, fsc, new_maps):
+    hbm = pl.BlockSpec(memory_space=pl.ANY)
+    vmem = pl.BlockSpec(memory_space=pltpu.VMEM)
+    return pl.pallas_call(
+        deliver_kernel,
+        out_shape=(
+            jax.ShapeDtypeStruct((1, PART), F32),
+            jax.ShapeDtypeStruct((NSHELL,), F32),
+            jax.ShapeDtypeStruct((ORI, ROWS, BOX), F32),
+        ),
+        in_specs=[vmem, vmem, hbm],
+        out_specs=(vmem, vmem, hbm),
+        scratch_shapes=[pltpu.SemaphoreType.DMA((DELIVER,))],
+        compiler_params=pltpu.CompilerParams(vmem_limit_bytes=60 * 1024 * 1024),
+        name="deliver",
+    )(scores, fsc, new_maps)
 
 
 def run_main(*operands):
@@ -618,7 +668,7 @@
             jax.ShapeDtypeStruct((ORI, ROWS, BOX), F32),
         ),
         in_specs=[hbm] * 15,
-        out_specs=(vmem, vmem, vmem),
+        out_specs=(vmem, vmem, pl.BlockSpec(memory_space=pl.ANY)),
         scratch_shapes=[
             smem((PART,), I32), smem((2, PART), I32), smem((PART,), I32), smem((CLASSES,), F32),
             smem((512,), I32),
@@ -650,13 +700,14 @@
             smem((4, 4, 1, 128), I32),
             v((SLOTS, 128), I32),
             smem((SLOTS, 128), I32),
-            v((8, 8, SHELLS), F32),
-            v((4, 8, SHELLS), F32),
-            v((8, 8, SHELLS), F32),
-            v((3, 8, SHELLS), F32),
+            v((ORI, ROWS, BOX), F32),
+            v((8, 1, 3 * SHELLS), F32),
+            v((4, 1, 3 * SHELLS), F32),
+            v((8, 1, 3 * SHELLS), F32),
+            v((3, 1, 3 * SHELLS), F32),
             v((SLABS, ROWS, 4 * BOX), BF16),
-            v((SLABS, 40, 128), F32),
-            v((SLABS, 40, 128), F32),
+            v((SLABS, 48, 128), BF16),
+            v((SLABS, 48, 128), BF16),
             v((DOMS, 1, 128), F32),
             v((1, 128), F32),
             dma((15,)),
@@ -673,6 +724,7 @@
             dma((8,)), dma((8,)),
             dma((8,)), dma((8,)),
             dma((16,)), dma((16,)),
+            dma((4,)),
         ],
         compiler_params=pltpu.CompilerParams(
             collective_id=0, has_side_effects=True, vmem_limit_bytes=60 * 1024 * 1024
@@ -685,7 +737,8 @@
     scores, fsc, new_maps = run_main(
         orientation[0], offsets[0].T, defocus_class[0], defocus, ori_slot, images[0], half_maps[0], *consts
     )
-    return scores, new_maps[None], fsc[0, :NSHELL]
+    scores, fsc, new_maps = deliver(scores, fsc, new_maps)
+    return scores, new_maps[None], fsc
 
 
 def solution(mesh):

time: 65.7 us -> 125 us (1.90)
  Pallas kernels: 59.4 us -> 123 us
  local copies, waits for them, and re-layouts: 5.54 us -> 0 us
    pallas_call x0 -> x1, Pallas kernels: none -> 73.9 us  [deliver(): pl.pallas_call(deliver_kernel, out_shape=(jax.ShapeDtypeStruct((1, PART),...]
    pallas_call x1, Pallas kernels: 59.4 us -> 49.5 us  [run_main(): pl.pallas_call(main_kernel, out_shape=(jax.ShapeDtypeStruct((1, PART), F3...]
    unnamed x2 -> x0, local copies, waits for them, and re-layouts: 4.34 us -> none
where the time goes in v3:
time: 125 us; the launch traced here: 124 us
  Pallas kernels  123 us (98%)
    pallas_call x1, Pallas kernels, deliver(): pl.pallas_call(deliver_kernel, out_shape=(jax.ShapeDtypeStruct((1, PART),...  73.9 us
    pallas_call x1, Pallas kernels, run_main(): pl.pallas_call(main_kernel, out_shape=(jax.ShapeDtypeStruct((1, PART), F3...  49.5 us

profile of v3, /device:TPU:16, one launch (start us, length us, event | category | flops | bytes accessed | tf_op | source)
XLA Modules:
  0.0 124.1 jit_solution(8784589784382816306)
XLA Ops:
  0.6 49.5 %refine.1 = (f32[1,8]{1,0:T(1,128)}, f32[1,384]{1,0:T(1,128)}, f32[32,48,384]{2,1,0:T(8,128)}) custom-call(s32[8]{0:T(128)} %bitcast.11, s32[2,8]{1,0:T(2,128)} %bitcast.10, s32[8]{0:T(128)} %bitcast.12, f32[16]{0:T(128)} %defocus_hbm.1, s32[512]{0:T(512)} %slot_hbm.1, bf16[8,48,384]{2,1,0:T(8,128)(2,1)} %bitcast.9, bf16[32,48,384]{2,1,0:T(8,128)(2,1)} %bitcast.8, ...), custom_call_target="tpu_custom_call" | custom-call | tf_op jit(solution)/shard_map/refine/pallas_call | solution.py:663
  50.2 73.9 %deliver.1 = (f32[1,8]{1,0:T(1,128)}, f32[267]{0:T(512)}, f32[32,48,384]{2,1,0:T(8,128)}) custom-call(f32[1,8]{1,0:T(1,128)} %get-tuple-element.9.score_in, f32[1,384]{1,0:T(1,128)} %get-tuple-element.10.corr_in, f32[32,48,384]{2,1,0:T(8,128)} %get-tuple-element.11.new_in), custom_call_target="tpu_custom_call" | custom-call | tf_op jit(solution)/shard_map/deliver/pallas_call | solution.py:642

commit v4 on v3

--- a/solution.py
+++ b/solution.py
@@ -622,17 +622,22 @@
 DELIVER = 8
 
 
-def deliver_kernel(score_in, corr_in, new_in, score_out, corr_out, new_out, sem):
+def deliver_kernel(score_in, corr_in, new_in, score_out, corr_out, new_out, hold, in_sem, out_sem):
     step = ORI // DELIVER
-    copies = []
+    reads = []
+    writes = []
     for t in range(DELIVER):
         block = pl.ds(step * t, step)
-        copies.append(pltpu.make_async_copy(new_in.at[block], new_out.at[block], sem.at[t]))
-    for copy in copies:
+        reads.append(pltpu.make_async_copy(new_in.at[block], hold.at[block], in_sem.at[t]))
+        writes.append(pltpu.make_async_copy(hold.at[block], new_out.at[block], out_sem.at[t]))
+    for copy in reads:
         copy.start()
     score_out[...] = score_in[...]
     corr_out[...] = corr_in[0, :NSHELL]
-    for copy in copies:
+    for t in range(DELIVER):
+        reads[t].wait()
+        writes[t].start()
+    for copy in writes:
         copy.wait()
 
 
@@ -648,7 +653,11 @@
         ),
         in_specs=[vmem, vmem, hbm],
         out_specs=(vmem, vmem, hbm),
-        scratch_shapes=[pltpu.SemaphoreType.DMA((DELIVER,))],
+        scratch_shapes=[
+            pltpu.VMEM((ORI, ROWS, BOX), F32),
+            pltpu.SemaphoreType.DMA((DELIVER,)),
+            pltpu.SemaphoreType.DMA((DELIVER,)),
+        ],
         compiler_params=pltpu.CompilerParams(vmem_limit_bytes=60 * 1024 * 1024),
         name="deliver",
     )(scores, fsc, new_maps)

time: 125 us -> 54.7 us (0.44)
  Pallas kernels: 123 us -> 53.3 us
    pallas_call x1, Pallas kernels: 73.9 us -> 3.74 us  [deliver(): pl.pallas_call(deliver_kernel, out_shape=(jax.ShapeDtypeStruct((1, PART),...]
where the time goes in v4:
time: 54.7 us; the launch traced here: 53.9 us
  Pallas kernels  53.3 us (97%)
  between operations  0.64 us (1%)
    pallas_call x1, Pallas kernels, run_main(): pl.pallas_call(main_kernel, out_shape=(jax.ShapeDtypeStruct((1, PART), F3...  49.5 us
    pallas_call x1, Pallas kernels, deliver(): pl.pallas_call(deliver_kernel, out_shape=(jax.ShapeDtypeStruct((1, PART),...  3.74 us

profile of v4, /device:TPU:16, one launch (start us, length us, event | category | flops | bytes accessed | tf_op | source)
XLA Modules:
  0.0 53.9 jit_solution(2923597009630713526)
XLA Ops:
  0.6 49.5 %refine.1 = (f32[1,8]{1,0:T(1,128)}, f32[1,384]{1,0:T(1,128)}, f32[32,48,384]{2,1,0:T(8,128)}) custom-call(s32[8]{0:T(128)} %bitcast.11, s32[2,8]{1,0:T(2,128)} %bitcast.10, s32[8]{0:T(128)} %bitcast.12, f32[16]{0:T(128)} %defocus_hbm.1, s32[512]{0:T(512)} %slot_hbm.1, bf16[8,48,384]{2,1,0:T(8,128)(2,1)} %bitcast.9, bf16[32,48,384]{2,1,0:T(8,128)(2,1)} %bitcast.8, ...), custom_call_target="tpu_custom_call" | custom-call | tf_op jit(solution)/shard_map/refine/pallas_call | solution.py:672
  50.2 3.7 %deliver.1 = (f32[1,8]{1,0:T(1,128)}, f32[267]{0:T(512)}, f32[32,48,384]{2,1,0:T(8,128)}) custom-call(f32[1,8]{1,0:T(1,128)} %get-tuple-element.9.score_in, f32[1,384]{1,0:T(1,128)} %get-tuple-element.10.corr_in, f32[32,48,384]{2,1,0:T(8,128)} %get-tuple-element.11.new_in), custom_call_target="tpu_custom_call" | custom-call | tf_op jit(solution)/shard_map/deliver/pallas_call | solution.py:647

commit v5 on v3

--- a/solution.py
+++ b/solution.py
@@ -118,17 +118,17 @@
 def main_kernel(
     ori_hbm, off_hbm, cls_hbm, defocus_hbm, slot_hbm, img_hbm, map_hbm,
     shell_hbm, ends_hbm, freq_hbm, tx_hbm, ty_hbm, col_hbm, rowt_hbm, tri_hbm,
-    score_ref, corr_ref, new_hbm,
+    score_ref, corr_ref, new_ref,
     ori_ref, off_ref, cls_ref, defocus_ref, slot_ref,
     img, maps, other, shell_of, ends, freq, tx, ty, col, rowt, tri, weight_ref,
     packed, stage, regular, extra, contrib, vprod, eprod, ctf, eyb,
     meta_out, meta_stage, meta_in, meta_own, meta_all, link_v, link,
-    new_ref, ar1, ar2, ar3, arx, prod, part, parts_in, ret, ret_out,
+    ar1, ar2, ar3, arx, prod, part, parts_in, ret, ret_out,
     load_sem, own_sem, ring_sem, map_send, map_recv,
     img1_send, img1_recv, img2_send, img2_recv, ext_send, ext_recv,
     meta1_send, meta1_recv, meta2_send, meta2_recv,
     ar1_send, ar1_recv, ar2_send, ar2_recv, ar3_send, ar3_recv,
-    part_send, part_recv, ret_send, ret_recv, new_sem,
+    part_send, part_recv, ret_send, ret_recv,
 ):
     h = lax.axis_index("half")
     d = lax.axis_index("dom")
@@ -587,13 +587,7 @@
         new_ref[r] = top / (has * eprod[at] + inverse)
         return carry
 
-    new_copies = []
-    for t in range(4):
-        lax.fori_loop(8 * t, 8 * t + 8, one_slice, 0)
-        block = pl.ds(8 * t, 8)
-        copy = pltpu.make_async_copy(new_ref.at[block], new_hbm.at[block], new_sem.at[t])
-        copy.start()
-        new_copies.append(copy)
+    lax.fori_loop(0, ORI, one_slice, 0)
 
     for r in range(DOMS):
         s = (d + r) % DOMS
@@ -615,8 +609,6 @@
         for r in FAR8:
             score_copy(e, r).wait_send()
         pl.when(2 * z + e != d)(score_copy(e, 0).wait_send)
-    for copy in new_copies:
-        copy.wait()
 
 
 DELIVER = 8
@@ -624,15 +616,15 @@
 
 def deliver_kernel(score_in, corr_in, new_in, score_out, corr_out, new_out, sem):
     step = ORI // DELIVER
-    copies = []
+    writes = []
     for t in range(DELIVER):
         block = pl.ds(step * t, step)
-        copies.append(pltpu.make_async_copy(new_in.at[block], new_out.at[block], sem.at[t]))
-    for copy in copies:
+        writes.append(pltpu.make_async_copy(new_in.at[block], new_out.at[block], sem.at[t]))
+    for copy in writes:
         copy.start()
     score_out[...] = score_in[...]
     corr_out[...] = corr_in[0, :NSHELL]
-    for copy in copies:
+    for copy in writes:
         copy.wait()
 
 
@@ -646,10 +638,12 @@
             jax.ShapeDtypeStruct((NSHELL,), F32),
             jax.ShapeDtypeStruct((ORI, ROWS, BOX), F32),
         ),
-        in_specs=[vmem, vmem, hbm],
+        in_specs=[vmem, vmem, vmem],
         out_specs=(vmem, vmem, hbm),
-        scratch_shapes=[pltpu.SemaphoreType.DMA((DELIVER,))],
-        compiler_params=pltpu.CompilerParams(vmem_limit_bytes=60 * 1024 * 1024),
+        scratch_shapes=[
+            pltpu.SemaphoreType.DMA((DELIVER,)),
+        ],
+        compiler_params=pltpu.CompilerParams(vmem_limit_bytes=16 * 1024 * 1024),
         name="deliver",
     )(scores, fsc, new_maps)
 
@@ -663,12 +657,12 @@
     return pl.pallas_call(
         main_kernel,
         out_shape=(
-            jax.ShapeDtypeStruct((1, PART), F32),
-            jax.ShapeDtypeStruct((1, SHELLS), F32),
-            jax.ShapeDtypeStruct((ORI, ROWS, BOX), F32),
+            pltpu.VMEM((1, PART), F32),
+            pltpu.VMEM((1, SHELLS), F32),
+            pltpu.VMEM((ORI, ROWS, BOX), F32),
         ),
         in_specs=[hbm] * 15,
-        out_specs=(vmem, vmem, pl.BlockSpec(memory_space=pl.ANY)),
+        out_specs=(vmem, vmem, vmem),
         scratch_shapes=[
             smem((PART,), I32), smem((2, PART), I32), smem((PART,), I32), smem((CLASSES,), F32),
             smem((512,), I32),
@@ -700,7 +694,6 @@
             smem((4, 4, 1, 128), I32),
             v((SLOTS, 128), I32),
             smem((SLOTS, 128), I32),
-            v((ORI, ROWS, BOX), F32),
             v((8, 1, 3 * SHELLS), F32),
             v((4, 1, 3 * SHELLS), F32),
             v((8, 1, 3 * SHELLS), F32),
@@ -724,13 +717,12 @@
             dma((8,)), dma((8,)),
             dma((8,)), dma((8,)),
             dma((16,)), dma((16,)),
-            dma((4,)),
         ],
         compiler_params=pltpu.CompilerParams(
-            collective_id=0, has_side_effects=True, vmem_limit_bytes=60 * 1024 * 1024
+            collective_id=0, has_side_effects=True, vmem_limit_bytes=44 * 1024 * 1024
         ),
         name="refine",
-    )(*operands)
+    )(*[pltpu.with_memory_space_constraint(x, pltpu.HBM) for x in operands])
 
 
 def on_device(consts, images, orientation, offsets, defocus_class, defocus, ori_slot, half_maps):

time: 125 us -> 52.3 us (0.42)
  Pallas kernels: 123 us -> 50.9 us
    pallas_call x1, Pallas kernels: 73.9 us -> 2.03 us  [deliver(): pl.pallas_call(deliver_kernel, out_shape=(jax.ShapeDtypeStruct((1, PART),...]
where the time goes in v5:
time: 52.3 us; the launch traced here: 51.6 us
  Pallas kernels  50.9 us (97%)
  between operations  0.64 us (1%)
    pallas_call x1, Pallas kernels, run_main(): pl.pallas_call(main_kernel, out_shape=(pltpu.VMEM((1, PART), F32), pltpu....  48.9 us
    pallas_call x1, Pallas kernels, deliver(): pl.pallas_call(deliver_kernel, out_shape=(jax.ShapeDtypeStruct((1, PART),...  2.03 us

profile of v5, /device:TPU:16, one launch (start us, length us, event | category | flops | bytes accessed | tf_op | source)
XLA Modules:
  0.0 51.6 jit_solution(3634842620199661695)
XLA Ops:
  0.6 48.9 %refine.1 = (f32[1,8]{1,0:T(1,128)S(1)}, f32[1,384]{1,0:T(1,128)S(1)}, f32[32,48,384]{2,1,0:T(8,128)S(1)}) custom-call(s32[8]{0:T(128)} %bitcast.11, s32[2,8]{1,0:T(2,128)} %bitcast.10, s32[8]{0:T(128)} %bitcast.12, f32[16]{0:T(128)} %defocus_hbm.1, s32[512]{0:T(512)} %slot_hbm.1, bf16[8,48,384]{2,1,0:T(8,128)(2,1)} %bitcast.9, ...), custom_call_target="tpu_custom_call" | custom-call | tf_op jit(solution)/shard_map/refine/pallas_call | solution.py:657
  49.5 2.0 %deliver.1 = (f32[1,8]{1,0:T(1,128)}, f32[267]{0:T(512)}, f32[32,48,384]{2,1,0:T(8,128)}) custom-call(f32[1,8]{1,0:T(1,128)S(1)} %get-tuple-element.9.score_in, f32[1,384]{1,0:T(1,128)S(1)} %get-tuple-element.10.corr_in, f32[32,48,384]{2,1,0:T(8,128)S(1)} %get-tuple-element.11.new_in), custom_call_target="tpu_custom_call" | custom-call | tf_op jit(solution)/shard_map/deliver/pallas_call | solution.py:634

commit v6 on v5

--- a/solution.py
+++ b/solution.py
@@ -151,14 +151,14 @@
     def signal(sem, where):
         pl.semaphore_signal(sem, inc=1, device_id=where, device_id_type=MESH)
 
+    neighbours = (
+        {"half": 1 - h}, {"half": 1 - h, "dom": y * 4 + flip(2)}, {"dom": y * 4 + flip(1)},
+        {"dom": (y + 1) % 4 * 4 + q}, {"dom": (y + 3) % 4 * 4 + q},
+        {"slab": (z + 1) % SLABS}, {"slab": (z + 7) % SLABS},
+    )
     barrier = pltpu.get_barrier_semaphore()
-    for r in FAR8:
-        to = (g + r) % 8
-        signal(barrier, {"half": to // 4, "dom": y * 4 + to % 4})
-    for r in FAR4:
-        signal(barrier, {"dom": (y + r) % 4 * 4 + q})
-    for r in (1, SLABS - 1):
-        signal(barrier, {"slab": (z + r) % SLABS})
+    for where in neighbours:
+        signal(barrier, where)
 
     loads = [
         (ori_hbm, ori_ref), (off_hbm, off_ref), (cls_hbm, cls_ref), (slot_hbm, slot_ref),
@@ -199,7 +199,7 @@
     own_copy = pltpu.make_async_copy(meta_out, meta_own, own_sem.at[0])
     own_copy.start()
 
-    pl.semaphore_wait(barrier, 7 + 3 + 2)
+    pl.semaphore_wait(barrier, len(neighbours))
 
     map_copies = []
     for c in range(NCHUNK):
@@ -212,10 +212,23 @@
     copies = list(map_copies)
 
     def ring(k):
-        for r in (1, SLABS - 1):
-            signal(ring_sem.at[k], {"slab": (z + r) % SLABS})
+        for where in neighbours:
+            signal(ring_sem.at[k], where)
 
     ring(0)
+
+    own_copy.wait()
+    ld_img.wait()
+
+    def pack(o, carry):
+        packed[o // 4, o % 4] = img[meta_own[o // 4, o % 4, 0, 5]]
+        return carry
+
+    lax.fori_loop(0, DOMS, pack, 0)
+    for t in range(4):
+        packed[t, 4] = img[second]
+    pl.semaphore_wait(ring_sem.at[0], len(neighbours))
+    ring(1)
 
     for r in FAR4:
         to = (y + r) % 4
@@ -224,16 +237,6 @@
         )
         copy.start()
         copies.append(copy)
-    own_copy.wait()
-    ld_img.wait()
-
-    def pack(o, carry):
-        packed[o // 4, o % 4] = img[meta_own[o // 4, o % 4, 0, 5]]
-        return carry
-
-    lax.fori_loop(0, DOMS, pack, 0)
-    for t in range(4):
-        packed[t, 4] = img[second]
     for r in FAR4:
         to = (y + r) % 4
         copy = remote(packed.at[to], stage.at[:, y], img1_send.at[r], img1_recv.at[y], {"dom": to * 4 + q})
@@ -243,8 +246,6 @@
     own_img.start()
     own_meta = pltpu.make_async_copy(meta_out.at[y], meta_stage.at[:, y], own_sem.at[2])
     own_meta.start()
-    pl.semaphore_wait(ring_sem.at[0], 2)
-    ring(1)
 
     ld_freq.wait()
     ld_defocus.wait()
@@ -254,7 +255,7 @@
         return carry
 
     lax.fori_loop(0, CLASSES, one_class, 0)
-    pl.semaphore_wait(ring_sem.at[1], 2)
+    pl.semaphore_wait(ring_sem.at[1], len(neighbours))
     ring(2)
     ld_ty.wait()
     for part_of in range(2):
@@ -282,7 +283,25 @@
         return total + m * m
 
     own_sq = lax.fori_loop(0, ORI, own_power, jnp.zeros((ROWS, BOX), F32))
-    pl.semaphore_wait(ring_sem.at[2], 2)
+    pl.semaphore_wait(ring_sem.at[2], len(neighbours))
+    ld_tri.wait()
+    ld_ends.wait()
+
+    def shell_sums(values):
+        running = jnp.dot(jnp.concatenate(split3(values), axis=0), tri[...], preferred_element_type=F32)
+        c = running[:ROWS] + (running[ROWS : 2 * ROWS] + running[2 * ROWS :])
+        blocks = []
+        for b in range(2):
+            e = ends[:, 128 * b : 128 * b + 128]
+            low = jnp.take_along_axis(c[:, :128], jnp.clip(e - 1, 0, 127), axis=1)
+            high = jnp.take_along_axis(c[:, 128:], jnp.clip(e - 129, 0, 127), axis=1)
+            got = jnp.where(e > 128, high, jnp.where(e > 0, low, 0.0))
+            blocks.append(jnp.sum(got, axis=0, keepdims=True))
+        first = blocks[0] - jnp.where(lane1 == 0, 0.0, pltpu.roll(blocks[0], 1, 1))
+        carry_in = jnp.where(lane1 == 0, blocks[0][:, 127:128], pltpu.roll(blocks[1], 1, 1))
+        return first, blocks[1] - carry_in
+
+    power_sums = shell_sums(own_sq)
     cross = jnp.zeros((ROWS, BOX), F32)
     for c in range(NCHUNK):
         if c == NCHUNK - 1:
@@ -319,25 +338,7 @@
         copy.start()
         copies.append(copy)
 
-    ld_tri.wait()
-    ld_ends.wait()
-    pieces = jnp.concatenate(list(split3(cross)) + list(split3(own_sq)), axis=0)
-    running = jnp.dot(pieces, tri[...], preferred_element_type=F32)
-    lane = lax.broadcasted_iota(I32, (1, 128), 1)
-    sums = []
-    for v in range(2):
-        o = 3 * ROWS * v
-        c = running[o : o + ROWS] + (running[o + ROWS : o + 2 * ROWS] + running[o + 2 * ROWS : o + 3 * ROWS])
-        blocks = []
-        for b in range(2):
-            e = ends[:, 128 * b : 128 * b + 128]
-            low = jnp.take_along_axis(c[:, :128], jnp.clip(e - 1, 0, 127), axis=1)
-            high = jnp.take_along_axis(c[:, 128:], jnp.clip(e - 129, 0, 127), axis=1)
-            got = jnp.where(e > 128, high, jnp.where(e > 0, low, 0.0))
-            blocks.append(jnp.sum(got, axis=0, keepdims=True))
-        first = blocks[0] - jnp.where(lane == 0, 0.0, pltpu.roll(blocks[0], 1, 1))
-        carry_in = jnp.where(lane == 0, blocks[0][:, 127:128], pltpu.roll(blocks[1], 1, 1))
-        sums.append((first, blocks[1] - carry_in))
+    sums = (shell_sums(cross), power_sums)
     shifted = (z == 3) | (z == 4)
     zero = jnp.zeros((1, 128), F32)
     for v in range(3):
@@ -497,40 +498,46 @@
         weight_ref[:, 128 * b : 128 * b + 128] = jnp.where(at < 128, low, high)
     w = weight_ref[...]
 
-    def weigh(t, carry):
-        energies = []
-        for k in range(4):
-            prod[t, :, BOX * k : BOX * k + BOX] = (vprod[4 * t + k] * w).astype(BF16)
-            e = jnp.sum(eprod[4 * t + k] * w, axis=0, keepdims=True)
-            energies.append(e[:, 0:128] + e[:, 128:256] + e[:, 256:384])
-        energies = jnp.concatenate(energies, axis=0)
-        part[t, 32:48, :] = jnp.concatenate(list(split3(energies)) + [jnp.zeros((4, 128), BF16)], axis=0)
-        return carry
-
-    lax.fori_loop(0, SLABS, weigh, 0)
     ld_col.wait()
     ld_rowt.wait()
-    section = jnp.dot(
-        prod[...].reshape(SLABS * ROWS, 4 * BOX), col[...], preferred_element_type=F32
-    ).astype(BF16)
-    stacked = jnp.concatenate(
-        [
-            jnp.concatenate(
-                [section[ROWS * t : ROWS * t + ROWS, :128], section[ROWS * t : ROWS * t + ROWS, 128:]], axis=0
-            )
-            for t in range(SLABS)
-        ],
-        axis=1,
-    )
-    partial = jnp.dot(rowt[...], stacked, preferred_element_type=F32)
-    for t in range(SLABS):
-        part[t, 0:32, :] = partial[:, 128 * t : 128 * t + 128].astype(BF16)
-
-    for r in FAR8:
-        to = (z + r) % SLABS
-        copy = remote(part.at[to], parts_in.at[z], part_send.at[r], part_recv.at[z], {"slab": to})
-        copy.start()
-        copies.append(copy)
+    for half, start in enumerate((3, 7)):
+
+        def weigh(j, carry):
+            t = (z + start + j) % SLABS
+            energies = []
+            for k in range(4):
+                prod[4 * half + j, :, BOX * k : BOX * k + BOX] = (vprod[4 * t + k] * w).astype(BF16)
+                e = jnp.sum(eprod[4 * t + k] * w, axis=0, keepdims=True)
+                energies.append(e[:, 0:128] + e[:, 128:256] + e[:, 256:384])
+            energies = jnp.concatenate(energies, axis=0)
+            part[t, 32:48, :] = jnp.concatenate(list(split3(energies)) + [jnp.zeros((4, 128), BF16)], axis=0)
+            return carry
+
+        lax.fori_loop(0, 4, weigh, 0)
+        section = jnp.dot(
+            prod[4 * half : 4 * half + 4].reshape(4 * ROWS, 4 * BOX), col[...], preferred_element_type=F32
+        ).astype(BF16)
+        stacked = jnp.concatenate(
+            [
+                jnp.concatenate(
+                    [section[ROWS * j : ROWS * j + ROWS, :128], section[ROWS * j : ROWS * j + ROWS, 128:]],
+                    axis=0,
+                )
+                for j in range(4)
+            ],
+            axis=1,
+        )
+        partial = jnp.dot(rowt[...], stacked, preferred_element_type=F32).astype(BF16)
+        for j in range(4):
+            part[(z + start + j) % SLABS, 0:32, :] = partial[:, 128 * j : 128 * j + 128]
+        for j in (1, 2, 0, 3):
+            r = (start + j) % SLABS
+            if r == 0:
+                continue
+            to = (z + r) % SLABS
+            copy = remote(part.at[to], parts_in.at[z], part_send.at[r], part_recv.at[z], {"slab": to})
+            copy.start()
+            copies.append(copy)
 
     link_copy.wait()
 
@@ -554,12 +561,12 @@
         remote(part.at[s], parts_in.at[s], part_send.at[r], part_recv.at[s], {"slab": s}).wait_recv()
         whole = whole + parts_in[s].astype(F32)
     best = jnp.max(whole[0:32], axis=0, keepdims=True)
-    answer = jnp.zeros((1, 128), F32)
-    for k in range(4):
-        top = jnp.max(jnp.where(lane1 // 32 == k, best, -jnp.inf), axis=1, keepdims=True)
-        energy = whole[32 + k : 33 + k] + (whole[36 + k : 37 + k] + whole[40 + k : 41 + k])
-        energy = jnp.sum(energy, axis=1, keepdims=True)
-        answer = jnp.where(lane1 == k, top / jnp.sqrt(energy + 1e-06), answer)
+    lane4 = lax.broadcasted_iota(I32, (4, 128), 1)
+    row4 = lax.broadcasted_iota(I32, (4, 128), 0)
+    top = jnp.max(jnp.where(lane4 // 32 == row4, best, -jnp.inf), axis=1, keepdims=True)
+    energy = jnp.sum(whole[32:36] + (whole[36:40] + whole[40:44]), axis=1, keepdims=True)
+    value = top / jnp.sqrt(energy + 1e-06)
+    answer = jnp.sum(jnp.where(lane4 == row4, value, 0.0), axis=0, keepdims=True)
     ret_out[...] = answer
 
     def score_copy(e, r):
@@ -589,6 +596,12 @@
 
     lax.fori_loop(0, ORI, one_slice, 0)
 
+    for copy in copies:
+        copy.wait_send()
+    for e in range(2):
+        for r in FAR8:
+            score_copy(e, r).wait_send()
+        pl.when(2 * z + e != d)(score_copy(e, 0).wait_send)
     for r in range(DOMS):
         s = (d + r) % DOMS
         copy = remote(ret_out, ret.at[s], ret_send.at[r], ret_recv.at[s], {"dom": s, "slab": d // 2})
@@ -596,19 +609,12 @@
             pl.when(d // 2 != z)(copy.wait_recv)
         else:
             copy.wait_recv()
-    scores = jnp.zeros((1, 128), F32)
-    for p in range(PART):
-        row = ret[owners[p]]
-        value = jnp.sum(jnp.where(lane1 == 2 * (d % 2) + ranks[p], row, 0.0), axis=1, keepdims=True)
-        scores = jnp.where(lane1 == p, value, scores)
+    picked = [jnp.where(lane1 == 2 * (d % 2) + ranks[p], ret[owners[p]], 0.0) for p in range(PART)]
+    picked = jnp.sum(jnp.concatenate(picked, axis=0), axis=1, keepdims=True)
+    lane8 = lax.broadcasted_iota(I32, (PART, 128), 1)
+    row8 = lax.broadcasted_iota(I32, (PART, 128), 0)
+    scores = jnp.sum(jnp.where(lane8 == row8, picked, 0.0), axis=0, keepdims=True)
     score_ref[...] = scores[:, :PART]
-
-    for copy in copies:
-        copy.wait_send()
-    for e in range(2):
-        for r in FAR8:
-            score_copy(e, r).wait_send()
-        pl.when(2 * z + e != d)(score_copy(e, 0).wait_send)
 
 
 DELIVER = 8

time: 52.3 us -> 50.5 us (0.966)
  Pallas kernels: 50.9 us -> 49.6 us
    pallas_call x1, Pallas kernels: 48.9 us -> 47.6 us  [run_main(): pl.pallas_call(main_kernel, out_shape=(pltpu.VMEM((1, PART), F32), pltpu....]
where the time goes in v6:
time: 50.5 us; the launch traced here: 50.3 us
  Pallas kernels  49.6 us (98%)
  between operations  0.64 us (1%)
    pallas_call x1, Pallas kernels, run_main(): pl.pallas_call(main_kernel, out_shape=(pltpu.VMEM((1, PART), F32), pltpu....  47.6 us
    pallas_call x1, Pallas kernels, deliver(): pl.pallas_call(deliver_kernel, out_shape=(jax.ShapeDtypeStruct((1, PART),...  2.03 us

profile of v6, /device:TPU:16, one launch (start us, length us, event | category | flops | bytes accessed | tf_op | source)
XLA Modules:
  0.0 50.3 jit_solution(3527997794299902015)
XLA Ops:
  0.6 47.6 %refine.1 = (f32[1,8]{1,0:T(1,128)S(1)}, f32[1,384]{1,0:T(1,128)S(1)}, f32[32,48,384]{2,1,0:T(8,128)S(1)}) custom-call(s32[8]{0:T(128)} %bitcast.11, s32[2,8]{1,0:T(2,128)} %bitcast.10, s32[8]{0:T(128)} %bitcast.12, f32[16]{0:T(128)} %defocus_hbm.1, s32[512]{0:T(512)} %slot_hbm.1, bf16[8,48,384]{2,1,0:T(8,128)(2,1)} %bitcast.9, ...), custom_call_target="tpu_custom_call" | custom-call | tf_op jit(solution)/shard_map/refine/pallas_call | solution.py:663
  48.3 2.0 %deliver.1 = (f32[1,8]{1,0:T(1,128)}, f32[267]{0:T(512)}, f32[32,48,384]{2,1,0:T(8,128)}) custom-call(f32[1,8]{1,0:T(1,128)S(1)} %get-tuple-element.9.score_in, f32[1,384]{1,0:T(1,128)S(1)} %get-tuple-element.10.corr_in, f32[32,48,384]{2,1,0:T(8,128)S(1)} %get-tuple-element.11.new_in), custom_call_target="tpu_custom_call" | custom-call | tf_op jit(solution)/shard_map/deliver/pallas_call | solution.py:640

commit v7 on v6

--- a/solution.py
+++ b/solution.py
@@ -123,11 +123,11 @@
     img, maps, other, shell_of, ends, freq, tx, ty, col, rowt, tri, weight_ref,
     packed, stage, regular, extra, contrib, vprod, eprod, ctf, eyb,
     meta_out, meta_stage, meta_in, meta_own, meta_all, link_v, link,
-    ar1, ar2, ar3, arx, prod, part, parts_in, ret, ret_out,
+    ar1, ar2, arx, prod, part, parts_in, ret, ret_out,
     load_sem, own_sem, ring_sem, map_send, map_recv,
     img1_send, img1_recv, img2_send, img2_recv, ext_send, ext_recv,
     meta1_send, meta1_recv, meta2_send, meta2_recv,
-    ar1_send, ar1_recv, ar2_send, ar2_recv, ar3_send, ar3_recv,
+    ar1_send, ar1_recv, ar2_send, ar2_recv,
     part_send, part_recv, ret_send, ret_recv,
 ):
     h = lax.axis_index("half")
@@ -135,7 +135,6 @@
     z = lax.axis_index("slab")
     y = d // 4
     q = d % 4
-    g = h * 4 + q
 
     def flip(bits):
         hi = (q // 2 + bits // 2) % 2
@@ -156,6 +155,37 @@
         {"dom": (y + 1) % 4 * 4 + q}, {"dom": (y + 3) % 4 * 4 + q},
         {"slab": (z + 1) % SLABS}, {"slab": (z + 7) % SLABS},
     )
+    core = q % 2
+    place_x = q // 2 * 2 + h
+    along_z = []
+    for r in (4, 3, 5, 2, 6, 1, 7, 0):
+        for c in (1, 0):
+            if r or c:
+                to_z, to_core = (z + r) % SLABS, (core + c) % 2
+                where = {"slab": to_z, "dom": y * 4 + q // 2 * 2 + to_core}
+                along_z.append((where, z * 2 + core, to_z * 2 + to_core))
+    in_plane = []
+    for r in (2, 1, 3, 0):
+        for c in (2, 1, 3, 0):
+            if r or c:
+                to_y, to_x = (y + r) % 4, (place_x + c) % 4
+                where = {"half": to_x % 2, "dom": to_y * 4 + to_x // 2 * 2 + core}
+                in_plane.append((where, y * 4 + place_x, to_y * 4 + to_x))
+
+    def spread(source, peers, landing, sends, receives):
+        for i, (where, mine, _) in enumerate(peers):
+            copy = remote(source, landing.at[mine], sends.at[i], receives.at[mine], where)
+            copy.start()
+            copies.append(copy)
+
+    def gather(source, peers, landing, sends, receives):
+        for i, (where, _, theirs) in reversed(list(enumerate(peers))):
+            remote(source, landing.at[theirs], sends.at[i], receives.at[theirs], where).wait_recv()
+        total = landing[0]
+        for i in range(1, 16):
+            total = total + landing[i]
+        return total
+
     barrier = pltpu.get_barrier_semaphore()
     for where in neighbours:
         signal(barrier, where)
@@ -284,6 +314,7 @@
 
     own_sq = lax.fori_loop(0, ORI, own_power, jnp.zeros((ROWS, BOX), F32))
     pl.semaphore_wait(ring_sem.at[2], len(neighbours))
+    ring(3)
     ld_tri.wait()
     ld_ends.wait()
 
@@ -338,6 +369,8 @@
         copy.start()
         copies.append(copy)
 
+    pl.semaphore_wait(ring_sem.at[3], len(neighbours))
+
     sums = (shell_sums(cross), power_sums)
     shifted = (z == 3) | (z == 4)
     zero = jnp.zeros((1, 128), F32)
@@ -349,11 +382,8 @@
                 block = jnp.where(h == v - 1, block, zero)
             arx[0, :, SHELLS * v + 128 * b : SHELLS * v + 128 * b + 128] = block
 
-    for r in FAR8:
-        to = (z + r) % SLABS
-        copy = remote(arx.at[0], ar1.at[z], ar1_send.at[r], ar1_recv.at[z], {"slab": to})
-        copy.start()
-        copies.append(copy)
+    spread(arx.at[0], along_z, ar1, ar1_send, ar1_recv)
+    ar1[z * 2 + core] = arx[0]
 
     last_meta.wait()
     for bits in (1, 2, 3):
@@ -429,42 +459,18 @@
     items_of(extra, q, 1)
     wait_extra(1)
     items_of(extra, flip(1), 1)
-    ar1[z] = arx[0]
-    for r in NEAR8:
-        s = (z + r) % SLABS
-        remote(arx.at[0], ar1.at[s], ar1_send.at[r], ar1_recv.at[s], {"slab": s}).wait_recv()
-    total = ar1[0]
-    for s in range(1, SLABS):
-        total = total + ar1[s]
-    arx[1] = total
-    for r in FAR4:
-        to = (y + r) % 4
-        copy = remote(arx.at[1], ar2.at[y], ar2_send.at[r], ar2_recv.at[y], {"dom": to * 4 + q})
-        copy.start()
-        copies.append(copy)
     wait_regular(1)
     items_of(regular, flip(1), 0)
+    total = gather(arx.at[0], along_z, ar1, ar1_send, ar1_recv)
+    arx[1] = total
+    spread(arx.at[1], in_plane, ar2, ar2_send, ar2_recv)
+    ar2[y * 4 + place_x] = total
     wait_extra(2)
     copy = remote(
         extra.at[flip(2)], extra.at[flip(2)], ext_send.at[3], ext_recv.at[flip(2)], {"dom": y * 4 + flip(1)}
     )
     copy.start()
     copies.append(copy)
-    ar2[y] = total
-    for r in NEAR4:
-        s = (y + r) % 4
-        remote(arx.at[1], ar2.at[s], ar2_send.at[r], ar2_recv.at[s], {"dom": s * 4 + q}).wait_recv()
-    total = ar2[0]
-    for s in range(1, 4):
-        total = total + ar2[s]
-    arx[2] = total
-    for r in FAR8:
-        to = (g + r) % 8
-        copy = remote(
-            arx.at[2], ar3.at[g], ar3_send.at[r], ar3_recv.at[g], {"half": to // 4, "dom": y * 4 + to % 4}
-        )
-        copy.start()
-        copies.append(copy)
     items_of(extra, flip(2), 1)
     wait_regular(2)
     items_of(regular, flip(2), 0)
@@ -472,19 +478,11 @@
     items_of(extra, flip(3), 1)
     wait_regular(3)
     items_of(regular, flip(3), 0)
-    ar3[g] = total
-    for r in NEAR8:
-        s = (g + r) % 8
-        remote(
-            arx.at[2], ar3.at[s], ar3_send.at[r], ar3_recv.at[s], {"half": s // 4, "dom": y * 4 + s % 4}
-        ).wait_recv()
-    total = ar3[0]
-    for s in range(1, 8):
-        total = total + ar3[s]
+    total = gather(arx.at[1], in_plane, ar2, ar2_send, ar2_recv)
 
     power = total[:, SHELLS : 2 * SHELLS] * total[:, 2 * SHELLS : 3 * SHELLS]
     fsc = total[:, :SHELLS] / jnp.sqrt(power + 1e-06)
-    corr_ref[...] = fsc
+    corr_ref[...] = fsc[0, :NSHELL]
     floor = jnp.maximum(fsc, 0.1)
     table0 = jnp.where(shifted, floor[:, 128:256], floor[:, 0:128])
     table1 = jnp.where(shifted, floor[:, 256:384], floor[:, 128:256])
@@ -626,10 +624,10 @@
     for t in range(DELIVER):
         block = pl.ds(step * t, step)
         writes.append(pltpu.make_async_copy(new_in.at[block], new_out.at[block], sem.at[t]))
+    writes.append(pltpu.make_async_copy(score_in, score_out, sem.at[DELIVER]))
+    writes.append(pltpu.make_async_copy(corr_in, corr_out, sem.at[DELIVER + 1]))
     for copy in writes:
         copy.start()
-    score_out[...] = score_in[...]
-    corr_out[...] = corr_in[0, :NSHELL]
     for copy in writes:
         copy.wait()
 
@@ -645,9 +643,9 @@
             jax.ShapeDtypeStruct((ORI, ROWS, BOX), F32),
         ),
         in_specs=[vmem, vmem, vmem],
-        out_specs=(vmem, vmem, hbm),
+        out_specs=(hbm, hbm, hbm),
         scratch_shapes=[
-            pltpu.SemaphoreType.DMA((DELIVER,)),
+            pltpu.SemaphoreType.DMA((DELIVER + 2,)),
         ],
         compiler_params=pltpu.CompilerParams(vmem_limit_bytes=16 * 1024 * 1024),
         name="deliver",
@@ -664,7 +662,7 @@
         main_kernel,
         out_shape=(
             pltpu.VMEM((1, PART), F32),
-            pltpu.VMEM((1, SHELLS), F32),
+            pltpu.VMEM((NSHELL,), F32),
             pltpu.VMEM((ORI, ROWS, BOX), F32),
         ),
         in_specs=[hbm] * 15,
@@ -700,10 +698,9 @@
             smem((4, 4, 1, 128), I32),
             v((SLOTS, 128), I32),
             smem((SLOTS, 128), I32),
-            v((8, 1, 3 * SHELLS), F32),
-            v((4, 1, 3 * SHELLS), F32),
-            v((8, 1, 3 * SHELLS), F32),
-            v((3, 1, 3 * SHELLS), F32),
+            v((16, 1, 3 * SHELLS), F32),
+            v((16, 1, 3 * SHELLS), F32),
+            v((2, 1, 3 * SHELLS), F32),
             v((SLABS, ROWS, 4 * BOX), BF16),
             v((SLABS, 48, 128), BF16),
             v((SLABS, 48, 128), BF16),
@@ -711,16 +708,15 @@
             v((1, 128), F32),
             dma((15,)),
             dma((8,)),
-            pltpu.SemaphoreType.REGULAR((3,)),
+            pltpu.SemaphoreType.REGULAR((4,)),
             dma((NCHUNK,)), dma((NCHUNK,)),
             dma((4,)), dma((4,)),
             dma((4,)), dma((4,)),
             dma((4,)), dma((4,)),
             dma((4,)), dma((4,)),
             dma((4,)), dma((4,)),
-            dma((8,)), dma((8,)),
-            dma((4,)), dma((4,)),
-            dma((8,)), dma((8,)),
+            dma((16,)), dma((16,)),
+            dma((16,)), dma((16,)),
             dma((8,)), dma((8,)),
             dma((16,)), dma((16,)),
         ],

time: 50.5 us -> 50.7 us (level)
    pallas_call x1, Pallas kernels: 47.6 us -> 48.3 us  [run_main(): pl.pallas_call(main_kernel, out_shape=(pltpu.VMEM((1, PART), F32), pltpu....]
    pallas_call x1, Pallas kernels: 2.03 us -> 1.49 us  [deliver(): pl.pallas_call(deliver_kernel, out_shape=(jax.ShapeDtypeStruct((1, PART),...]
where the time goes in v7:
time: 50.7 us; the launch traced here: 50.4 us
  Pallas kernels  49.8 us (98%)
  between operations  0.64 us (1%)
    pallas_call x1, Pallas kernels, run_main(): pl.pallas_call(main_kernel, out_shape=(pltpu.VMEM((1, PART), F32), pltpu....  48.3 us
    pallas_call x1, Pallas kernels, deliver(): pl.pallas_call(deliver_kernel, out_shape=(jax.ShapeDtypeStruct((1, PART),...  1.49 us

profile of v7, /device:TPU:16, one launch (start us, length us, event | category | flops | bytes accessed | tf_op | source)
XLA Modules:
  0.0 50.4 jit_solution(4670237292891090803)
XLA Ops:
  0.6 48.3 %refine.1 = (f32[1,8]{1,0:T(1,128)S(1)}, f32[267]{0:T(512)S(1)}, f32[32,48,384]{2,1,0:T(8,128)S(1)}) custom-call(s32[8]{0:T(128)} %bitcast.11, s32[2,8]{1,0:T(2,128)} %bitcast.10, s32[8]{0:T(128)} %bitcast.12, f32[16]{0:T(128)} %defocus_hbm.1, s32[512]{0:T(512)} %slot_hbm.1, bf16[8,48,384]{2,1,0:T(8,128)(2,1)} %bitcast.9, bf16[32,48,384]{2,1,0:T(8,128)(2,1)} %bitcast.8, ...), custom_call_target="tpu_custom_call" | custom-call | tf_op jit(solution)/shard_map/refine/pallas_call | solution.py:661
  48.9 1.5 %deliver.1 = (f32[1,8]{1,0:T(1,128)}, f32[267]{0:T(512)}, f32[32,48,384]{2,1,0:T(8,128)}) custom-call(f32[1,8]{1,0:T(1,128)S(1)} %get-tuple-element.9.score_in, f32[267]{0:T(512)S(1)} %get-tuple-element.10.corr_in, f32[32,48,384]{2,1,0:T(8,128)S(1)} %get-tuple-element.11.new_in), custom_call_target="tpu_custom_call" | custom-call | tf_op jit(solution)/shard_map/deliver/pallas_call | solution.py:638

commit v8 on v7

--- a/solution.py
+++ b/solution.py
@@ -363,11 +363,14 @@
     copy = remote(stage.at[4], extra.at[q], ext_send.at[2], ext_recv.at[q], {"dom": y * 4 + flip(2)})
     copy.start()
     copies.append(copy)
-    for bits in (2, 3):
+
+    def send_regular(bits):
         to = flip(bits)
         copy = remote(stage.at[to], regular.at[q], img2_send.at[bits], img2_recv.at[q], {"dom": y * 4 + to})
         copy.start()
         copies.append(copy)
+
+    send_regular(2)
 
     pl.semaphore_wait(ring_sem.at[3], len(neighbours))
 
@@ -464,6 +467,7 @@
     total = gather(arx.at[0], along_z, ar1, ar1_send, ar1_recv)
     arx[1] = total
     spread(arx.at[1], in_plane, ar2, ar2_send, ar2_recv)
+    send_regular(3)
     ar2[y * 4 + place_x] = total
     wait_extra(2)
     copy = remote(
@@ -476,8 +480,6 @@
     items_of(regular, flip(2), 0)
     wait_extra(3)
     items_of(extra, flip(3), 1)
-    wait_regular(3)
-    items_of(regular, flip(3), 0)
     total = gather(arx.at[1], in_plane, ar2, ar2_send, ar2_recv)
 
     power = total[:, SHELLS : 2 * SHELLS] * total[:, 2 * SHELLS : 3 * SHELLS]
@@ -496,12 +498,17 @@
         weight_ref[:, 128 * b : 128 * b + 128] = jnp.where(at < 128, low, high)
     w = weight_ref[...]
 
+    guarded = []
     ld_col.wait()
     ld_rowt.wait()
-    for half, start in enumerate((3, 7)):
+    for half in range(2):
+        from_x = (q // 2 + half) % 2
+        if half == 1:
+            wait_regular(3)
+            items_of(regular, flip(3), 0)
 
         def weigh(j, carry):
-            t = (z + start + j) % SLABS
+            t = 2 * j + from_x
             energies = []
             for k in range(4):
                 prod[4 * half + j, :, BOX * k : BOX * k + BOX] = (vprod[4 * t + k] * w).astype(BF16)
@@ -527,15 +534,16 @@
         )
         partial = jnp.dot(rowt[...], stacked, preferred_element_type=F32).astype(BF16)
         for j in range(4):
-            part[(z + start + j) % SLABS, 0:32, :] = partial[:, 128 * j : 128 * j + 128]
-        for j in (1, 2, 0, 3):
-            r = (start + j) % SLABS
+            part[2 * j + from_x, 0:32, :] = partial[:, 128 * j : 128 * j + 128]
+        for r in (2, 1, 3, 0):
+            to = 2 * ((z // 2 + r) % 4) + from_x
+            copy = remote(part.at[to], parts_in.at[z], part_send.at[to], part_recv.at[z], {"slab": to})
             if r == 0:
-                continue
-            to = (z + r) % SLABS
-            copy = remote(part.at[to], parts_in.at[z], part_send.at[r], part_recv.at[z], {"slab": to})
-            copy.start()
-            copies.append(copy)
+                pl.when(to != z)(copy.start)
+                guarded.append((to != z, copy))
+            else:
+                copy.start()
+                copies.append(copy)
 
     link_copy.wait()
 
@@ -596,6 +604,8 @@
 
     for copy in copies:
         copy.wait_send()
+    for sent, copy in guarded:
+        pl.when(sent)(copy.wait_send)
     for e in range(2):
         for r in FAR8:
             score_copy(e, r).wait_send()

time: 50.7 us -> 51.1 us (level)
  Pallas kernels: 49.8 us -> 50.4 us
    pallas_call x1, Pallas kernels: 48.3 us -> 48.9 us  [run_main(): pl.pallas_call(main_kernel, out_shape=(pltpu.VMEM((1, PART), F32), pltpu....]
where the time goes in v8:
time: 51.1 us; the launch traced here: 51 us
  Pallas kernels  50.4 us (99%)
  between operations  0.64 us (1%)
    pallas_call x1, Pallas kernels, run_main(): pl.pallas_call(main_kernel, out_shape=(pltpu.VMEM((1, PART), F32), pltpu....  48.9 us
    pallas_call x1, Pallas kernels, deliver(): pl.pallas_call(deliver_kernel, out_shape=(jax.ShapeDtypeStruct((1, PART),...  1.49 us

profile of v8, /device:TPU:16, one launch (start us, length us, event | category | flops | bytes accessed | tf_op | source)
XLA Modules:
  0.0 51.0 jit_solution(14112507809893906439)
XLA Ops:
  0.6 48.9 %refine.1 = (f32[1,8]{1,0:T(1,128)S(1)}, f32[267]{0:T(512)S(1)}, f32[32,48,384]{2,1,0:T(8,128)S(1)}) custom-call(s32[8]{0:T(128)} %bitcast.11, s32[2,8]{1,0:T(2,128)} %bitcast.10, s32[8]{0:T(128)} %bitcast.12, f32[16]{0:T(128)} %defocus_hbm.1, s32[512]{0:T(512)} %slot_hbm.1, bf16[8,48,384]{2,1,0:T(8,128)(2,1)} %bitcast.9, bf16[32,48,384]{2,1,0:T(8,128)(2,1)} %bitcast.8, ...), custom_call_target="tpu_custom_call" | custom-call | tf_op jit(solution)/shard_map/refine/pallas_call | solution.py:671
  49.5 1.5 %deliver.1 = (f32[1,8]{1,0:T(1,128)}, f32[267]{0:T(512)}, f32[32,48,384]{2,1,0:T(8,128)}) custom-call(f32[1,8]{1,0:T(1,128)S(1)} %get-tuple-element.9.score_in, f32[267]{0:T(512)S(1)} %get-tuple-element.10.corr_in, f32[32,48,384]{2,1,0:T(8,128)S(1)} %get-tuple-element.11.new_in), custom_call_target="tpu_custom_call" | custom-call | tf_op jit(solution)/shard_map/deliver/pallas_call | solution.py:648

commit v9 on v6

--- a/solution.py
+++ b/solution.py
@@ -332,11 +332,14 @@
     copy = remote(stage.at[4], extra.at[q], ext_send.at[2], ext_recv.at[q], {"dom": y * 4 + flip(2)})
     copy.start()
     copies.append(copy)
-    for bits in (2, 3):
+
+    def send_regular(bits):
         to = flip(bits)
         copy = remote(stage.at[to], regular.at[q], img2_send.at[bits], img2_recv.at[q], {"dom": y * 4 + to})
         copy.start()
         copies.append(copy)
+
+    send_regular(2)
 
     sums = (shell_sums(cross), power_sums)
     shifted = (z == 3) | (z == 4)
@@ -465,13 +468,12 @@
         )
         copy.start()
         copies.append(copy)
+    send_regular(3)
     items_of(extra, flip(2), 1)
     wait_regular(2)
     items_of(regular, flip(2), 0)
     wait_extra(3)
     items_of(extra, flip(3), 1)
-    wait_regular(3)
-    items_of(regular, flip(3), 0)
     ar3[g] = total
     for r in NEAR8:
         s = (g + r) % 8
@@ -484,7 +486,7 @@
 
     power = total[:, SHELLS : 2 * SHELLS] * total[:, 2 * SHELLS : 3 * SHELLS]
     fsc = total[:, :SHELLS] / jnp.sqrt(power + 1e-06)
-    corr_ref[...] = fsc
+    corr_ref[...] = fsc[0, :NSHELL]
     floor = jnp.maximum(fsc, 0.1)
     table0 = jnp.where(shifted, floor[:, 128:256], floor[:, 0:128])
     table1 = jnp.where(shifted, floor[:, 256:384], floor[:, 128:256])
@@ -498,12 +500,17 @@
         weight_ref[:, 128 * b : 128 * b + 128] = jnp.where(at < 128, low, high)
     w = weight_ref[...]
 
+    guarded = []
     ld_col.wait()
     ld_rowt.wait()
-    for half, start in enumerate((3, 7)):
+    for half in range(2):
+        from_x = (q // 2 + half) % 2
+        if half == 1:
+            wait_regular(3)
+            items_of(regular, flip(3), 0)
 
         def weigh(j, carry):
-            t = (z + start + j) % SLABS
+            t = 2 * j + from_x
             energies = []
             for k in range(4):
                 prod[4 * half + j, :, BOX * k : BOX * k + BOX] = (vprod[4 * t + k] * w).astype(BF16)
@@ -529,15 +536,16 @@
         )
         partial = jnp.dot(rowt[...], stacked, preferred_element_type=F32).astype(BF16)
         for j in range(4):
-            part[(z + start + j) % SLABS, 0:32, :] = partial[:, 128 * j : 128 * j + 128]
-        for j in (1, 2, 0, 3):
-            r = (start + j) % SLABS
+            part[2 * j + from_x, 0:32, :] = partial[:, 128 * j : 128 * j + 128]
+        for r in (2, 1, 3, 0):
+            to = 2 * ((z // 2 + r) % 4) + from_x
+            copy = remote(part.at[to], parts_in.at[z], part_send.at[to], part_recv.at[z], {"slab": to})
             if r == 0:
-                continue
-            to = (z + r) % SLABS
-            copy = remote(part.at[to], parts_in.at[z], part_send.at[r], part_recv.at[z], {"slab": to})
-            copy.start()
-            copies.append(copy)
+                pl.when(to != z)(copy.start)
+                guarded.append((to != z, copy))
+            else:
+                copy.start()
+                copies.append(copy)
 
     link_copy.wait()
 
@@ -598,6 +606,8 @@
 
     for copy in copies:
         copy.wait_send()
+    for sent, copy in guarded:
+        pl.when(sent)(copy.wait_send)
     for e in range(2):
         for r in FAR8:
             score_copy(e, r).wait_send()
@@ -626,10 +636,10 @@
     for t in range(DELIVER):
         block = pl.ds(step * t, step)
         writes.append(pltpu.make_async_copy(new_in.at[block], new_out.at[block], sem.at[t]))
+    writes.append(pltpu.make_async_copy(score_in, score_out, sem.at[DELIVER]))
+    writes.append(pltpu.make_async_copy(corr_in, corr_out, sem.at[DELIVER + 1]))
     for copy in writes:
         copy.start()
-    score_out[...] = score_in[...]
-    corr_out[...] = corr_in[0, :NSHELL]
     for copy in writes:
         copy.wait()
 
@@ -645,9 +655,9 @@
             jax.ShapeDtypeStruct((ORI, ROWS, BOX), F32),
         ),
         in_specs=[vmem, vmem, vmem],
-        out_specs=(vmem, vmem, hbm),
+        out_specs=(hbm, hbm, hbm),
         scratch_shapes=[
-            pltpu.SemaphoreType.DMA((DELIVER,)),
+            pltpu.SemaphoreType.DMA((DELIVER + 2,)),
         ],
         compiler_params=pltpu.CompilerParams(vmem_limit_bytes=16 * 1024 * 1024),
         name="deliver",
@@ -664,7 +674,7 @@
         main_kernel,
         out_shape=(
             pltpu.VMEM((1, PART), F32),
-            pltpu.VMEM((1, SHELLS), F32),
+            pltpu.VMEM((NSHELL,), F32),
             pltpu.VMEM((ORI, ROWS, BOX), F32),
         ),
         in_specs=[hbm] * 15,

time: 50.5 us -> 51.4 us (1.018)
  Pallas kernels: 49.6 us -> 50.6 us
    pallas_call x1, Pallas kernels: 47.6 us -> 49.1 us  [run_main(): pl.pallas_call(main_kernel, out_shape=(pltpu.VMEM((1, PART), F32), pltpu....]
    pallas_call x1, Pallas kernels: 2.03 us -> 1.49 us  [deliver(): pl.pallas_call(deliver_kernel, out_shape=(jax.ShapeDtypeStruct((1, PART),...]
where the time goes in v9:
time: 51.4 us; the launch traced here: 51.2 us
  Pallas kernels  50.6 us (98%)
  between operations  0.64 us (1%)
    pallas_call x1, Pallas kernels, run_main(): pl.pallas_call(main_kernel, out_shape=(pltpu.VMEM((1, PART), F32), pltpu....  49.1 us
    pallas_call x1, Pallas kernels, deliver(): pl.pallas_call(deliver_kernel, out_shape=(jax.ShapeDtypeStruct((1, PART),...  1.49 us

profile of v9, /device:TPU:16, one launch (start us, length us, event | category | flops | bytes accessed | tf_op | source)
XLA Modules:
  0.0 51.2 jit_solution(11599255740771154461)
XLA Ops:
  0.6 49.1 %refine.1 = (f32[1,8]{1,0:T(1,128)S(1)}, f32[267]{0:T(512)S(1)}, f32[32,48,384]{2,1,0:T(8,128)S(1)}) custom-call(s32[8]{0:T(128)} %bitcast.11, s32[2,8]{1,0:T(2,128)} %bitcast.10, s32[8]{0:T(128)} %bitcast.12, f32[16]{0:T(128)} %defocus_hbm.1, s32[512]{0:T(512)} %slot_hbm.1, bf16[8,48,384]{2,1,0:T(8,128)(2,1)} %bitcast.9, bf16[32,48,384]{2,1,0:T(8,128)(2,1)} %bitcast.8, ...), custom_call_target="tpu_custom_call" | custom-call | tf_op jit(solution)/shard_map/refine/pallas_call | solution.py:673
  49.7 1.5 %deliver.1 = (f32[1,8]{1,0:T(1,128)}, f32[267]{0:T(512)}, f32[32,48,384]{2,1,0:T(8,128)}) custom-call(f32[1,8]{1,0:T(1,128)S(1)} %get-tuple-element.9.score_in, f32[267]{0:T(512)S(1)} %get-tuple-element.10.corr_in, f32[32,48,384]{2,1,0:T(8,128)S(1)} %get-tuple-element.11.new_in), custom_call_target="tpu_custom_call" | custom-call | tf_op jit(solution)/shard_map/deliver/pallas_call | solution.py:650

commit v10 on v6

--- a/solution.py
+++ b/solution.py
@@ -484,7 +484,7 @@
 
     power = total[:, SHELLS : 2 * SHELLS] * total[:, 2 * SHELLS : 3 * SHELLS]
     fsc = total[:, :SHELLS] / jnp.sqrt(power + 1e-06)
-    corr_ref[...] = fsc
+    corr_ref[...] = fsc[0, :NSHELL]
     floor = jnp.maximum(fsc, 0.1)
     table0 = jnp.where(shifted, floor[:, 128:256], floor[:, 0:128])
     table1 = jnp.where(shifted, floor[:, 256:384], floor[:, 128:256])
@@ -626,10 +626,10 @@
     for t in range(DELIVER):
         block = pl.ds(step * t, step)
         writes.append(pltpu.make_async_copy(new_in.at[block], new_out.at[block], sem.at[t]))
+    writes.append(pltpu.make_async_copy(score_in, score_out, sem.at[DELIVER]))
+    writes.append(pltpu.make_async_copy(corr_in, corr_out, sem.at[DELIVER + 1]))
     for copy in writes:
         copy.start()
-    score_out[...] = score_in[...]
-    corr_out[...] = corr_in[0, :NSHELL]
     for copy in writes:
         copy.wait()
 
@@ -645,9 +645,9 @@
             jax.ShapeDtypeStruct((ORI, ROWS, BOX), F32),
         ),
         in_specs=[vmem, vmem, vmem],
-        out_specs=(vmem, vmem, hbm),
+        out_specs=(hbm, hbm, hbm),
         scratch_shapes=[
-            pltpu.SemaphoreType.DMA((DELIVER,)),
+            pltpu.SemaphoreType.DMA((DELIVER + 2,)),
         ],
         compiler_params=pltpu.CompilerParams(vmem_limit_bytes=16 * 1024 * 1024),
         name="deliver",
@@ -664,7 +664,7 @@
         main_kernel,
         out_shape=(
             pltpu.VMEM((1, PART), F32),
-            pltpu.VMEM((1, SHELLS), F32),
+            pltpu.VMEM((NSHELL,), F32),
             pltpu.VMEM((ORI, ROWS, BOX), F32),
         ),
         in_specs=[hbm] * 15,

time: 50.5 us -> 50 us (0.990)
    pallas_call x1, Pallas kernels: 2.03 us -> 1.49 us  [deliver(): pl.pallas_call(deliver_kernel, out_shape=(jax.ShapeDtypeStruct((1, PART),...]
where the time goes in v10:
time: 50 us; the launch traced here: 49.7 us
  Pallas kernels  49.1 us (98%)
  between operations  0.64 us (1%)
    pallas_call x1, Pallas kernels, run_main(): pl.pallas_call(main_kernel, out_shape=(pltpu.VMEM((1, PART), F32), pltpu....  47.6 us
    pallas_call x1, Pallas kernels, deliver(): pl.pallas_call(deliver_kernel, out_shape=(jax.ShapeDtypeStruct((1, PART),...  1.49 us

profile of v10, /device:TPU:16, one launch (start us, length us, event | category | flops | bytes accessed | tf_op | source)
XLA Modules:
  0.0 49.7 jit_solution(10042322084062251598)
XLA Ops:
  0.6 47.6 %refine.1 = (f32[1,8]{1,0:T(1,128)S(1)}, f32[267]{0:T(512)S(1)}, f32[32,48,384]{2,1,0:T(8,128)S(1)}) custom-call(s32[8]{0:T(128)} %bitcast.11, s32[2,8]{1,0:T(2,128)} %bitcast.10, s32[8]{0:T(128)} %bitcast.12, f32[16]{0:T(128)} %defocus_hbm.1, s32[512]{0:T(512)} %slot_hbm.1, bf16[8,48,384]{2,1,0:T(8,128)(2,1)} %bitcast.9, bf16[32,48,384]{2,1,0:T(8,128)(2,1)} %bitcast.8, ...), custom_call_target="tpu_custom_call" | custom-call | tf_op jit(solution)/shard_map/refine/pallas_call | solution.py:663
  48.3 1.5 %deliver.1 = (f32[1,8]{1,0:T(1,128)}, f32[267]{0:T(512)}, f32[32,48,384]{2,1,0:T(8,128)}) custom-call(f32[1,8]{1,0:T(1,128)S(1)} %get-tuple-element.9.score_in, f32[267]{0:T(512)S(1)} %get-tuple-element.10.corr_in, f32[32,48,384]{2,1,0:T(8,128)S(1)} %get-tuple-element.11.new_in), custom_call_target="tpu_custom_call" | custom-call | tf_op jit(solution)/shard_map/deliver/pallas_call | solution.py:640

commit v11 on v10

--- a/solution.py
+++ b/solution.py
@@ -500,22 +500,22 @@
 
     ld_col.wait()
     ld_rowt.wait()
-    for half, start in enumerate((3, 7)):
+    for half, start in enumerate((3, 5, 1, 7)):
 
         def weigh(j, carry):
             t = (z + start + j) % SLABS
             energies = []
             for k in range(4):
-                prod[4 * half + j, :, BOX * k : BOX * k + BOX] = (vprod[4 * t + k] * w).astype(BF16)
+                prod[2 * half + j, :, BOX * k : BOX * k + BOX] = (vprod[4 * t + k] * w).astype(BF16)
                 e = jnp.sum(eprod[4 * t + k] * w, axis=0, keepdims=True)
                 energies.append(e[:, 0:128] + e[:, 128:256] + e[:, 256:384])
             energies = jnp.concatenate(energies, axis=0)
             part[t, 32:48, :] = jnp.concatenate(list(split3(energies)) + [jnp.zeros((4, 128), BF16)], axis=0)
             return carry
 
-        lax.fori_loop(0, 4, weigh, 0)
+        lax.fori_loop(0, 2, weigh, 0)
         section = jnp.dot(
-            prod[4 * half : 4 * half + 4].reshape(4 * ROWS, 4 * BOX), col[...], preferred_element_type=F32
+            prod[2 * half : 2 * half + 2].reshape(2 * ROWS, 4 * BOX), col[...], preferred_element_type=F32
         ).astype(BF16)
         stacked = jnp.concatenate(
             [
@@ -523,14 +523,14 @@
                     [section[ROWS * j : ROWS * j + ROWS, :128], section[ROWS * j : ROWS * j + ROWS, 128:]],
                     axis=0,
                 )
-                for j in range(4)
+                for j in range(2)
             ],
             axis=1,
         )
         partial = jnp.dot(rowt[...], stacked, preferred_element_type=F32).astype(BF16)
-        for j in range(4):
+        for j in range(2):
             part[(z + start + j) % SLABS, 0:32, :] = partial[:, 128 * j : 128 * j + 128]
-        for j in (1, 2, 0, 3):
+        for j in (1, 0):
             r = (start + j) % SLABS
             if r == 0:
                 continue

time: 50 us -> 49.6 us (level)
  no operation moved by 1% of the time
where the time goes in v11:
time: 49.6 us; the launch traced here: 49.5 us
  Pallas kernels  48.8 us (98%)
  between operations  0.64 us (1%)
    pallas_call x1, Pallas kernels, run_main(): pl.pallas_call(main_kernel, out_shape=(pltpu.VMEM((1, PART), F32), pltpu....  47.4 us
    pallas_call x1, Pallas kernels, deliver(): pl.pallas_call(deliver_kernel, out_shape=(jax.ShapeDtypeStruct((1, PART),...  1.49 us

profile of v11, /device:TPU:16, one launch (start us, length us, event | category | flops | bytes accessed | tf_op | source)
XLA Modules:
  0.0 49.5 jit_solution(11765371436694495065)
XLA Ops:
  0.6 47.4 %refine.1 = (f32[1,8]{1,0:T(1,128)S(1)}, f32[267]{0:T(512)S(1)}, f32[32,48,384]{2,1,0:T(8,128)S(1)}) custom-call(s32[8]{0:T(128)} %bitcast.11, s32[2,8]{1,0:T(2,128)} %bitcast.10, s32[8]{0:T(128)} %bitcast.12, f32[16]{0:T(128)} %defocus_hbm.1, s32[512]{0:T(512)} %slot_hbm.1, bf16[8,48,384]{2,1,0:T(8,128)(2,1)} %bitcast.9, bf16[32,48,384]{2,1,0:T(8,128)(2,1)} %bitcast.8, ...), custom_call_target="tpu_custom_call" | custom-call | tf_op jit(solution)/shard_map/refine/pallas_call | solution.py:663
  48.0 1.5 %deliver.1 = (f32[1,8]{1,0:T(1,128)}, f32[267]{0:T(512)}, f32[32,48,384]{2,1,0:T(8,128)}) custom-call(f32[1,8]{1,0:T(1,128)S(1)} %get-tuple-element.9.score_in, f32[267]{0:T(512)S(1)} %get-tuple-element.10.corr_in, f32[32,48,384]{2,1,0:T(8,128)S(1)} %get-tuple-element.11.new_in), custom_call_target="tpu_custom_call" | custom-call | tf_op jit(solution)/shard_map/deliver/pallas_call | solution.py:640
